TPU v7x, 32 devices: a whole 2x2x4 slice. The times are simulated.
32 devices in a mesh: row: 4 (over y, x), col: 8 (over z, core).
Axes of the slice: x: 2, y: 2, z: 4, core: 2. Of those that a mesh axis runs over, the one named last changes fastest.
Arguments:
- pair_ints: bfloat16 [2048, 16384], P(None, ('row', 'col')), may hold values from -0.59765625 to 0.59765625
- denominators: float32 [2048], replicated, may hold values from 0.5 to 4
- lap_points: float32 [3], replicated, may hold values from 0.05 to 1.5
- lap_weights: float32 [3], replicated, may hold values from 0.2 to 1
Outputs:
- aux_matrices: float32 [3, 16384, 16384], P(None, 'row', 'col')
All inputs are finite; a program needn't handle non-finite values.
Results may differ from a plain program's by a relative error of at most 0.0027.
Values may be sent and summed in bfloat16 or wider, within the bound.
No kernel may reach another device: no remote copies, remote signals or barrier semaphores. Data moves between devices by JAX's collectives and lax.ppermute only.
A program may use at most 256 MiB of HBM per device.

v0:
```python
import jax
import jax.numpy as jnp
from jax import lax
from jax.sharding import PartitionSpec as P


def on_device(pair_ints, denominators, lap_points, lap_weights):
    factors = lap_weights[:, None] * jnp.exp(-lap_points[:, None] * denominators[None, :])
    pair_rows = lax.all_to_all(pair_ints, ("row", "col"), split_axis=0, concat_axis=1, tiled=True)
    col_block = lax.all_to_all(pair_rows, "col", split_axis=1, concat_axis=0, tiled=True)
    col_whole = lax.all_gather(col_block, "row", axis=0, tiled=True)
    weighted = (
        lax.all_gather(pair_ints, "col", axis=1, tiled=True).astype(jnp.float32)[None]
        * factors[:, :, None]
    ).astype(jnp.bfloat16)
    return jnp.einsum("trp,rq->tpq", weighted, col_whole, preferred_element_type=jnp.float32)


def solution(mesh):
    in_specs = (P(None, ("row", "col")), P(), P(), P())
    out_specs = P(None, "row", "col")
    return jax.shard_map(
        on_device, mesh=mesh, in_specs=in_specs, out_specs=out_specs, check_vma=False
    )
```

profile of v0, /device:TPU:31, one launch (start us, length us, event | category | flops | bytes accessed | tf_op | source)
XLA Modules:
  0.0 453.6 jit_solution(11565326096976383065)
XLA Ops:
  6.5 0.0 copy-start.2
  6.5 0.0 copy-start.1
  6.5 0.0 copy-start
  6.5 0.0 all-gather.3.cloned.1.call-start
  6.5 0.7 all-gather.3.cloned.1.call-update
  7.3 0.0 all-gather.5.cloned.1.call-start
  7.3 105.1 %all_to_all.35 = bf16[32,64,512]{2,1,0:T(8,128)(2,1)S(1)} all-to-all(bf16[32,64,512]{2,1,0:T(8,128)(2,1)} %bitcast.9), channel_id=1, replica_groups=mesh['row'=4,'col'=8] {'row','col'}, dimensions={0} | all-to-all | bytes 4194304 | tf_op jit(solution)/shard_map/all_to_all | solution.py:9
  112.4 1.2 copy.10
  113.6 2.6 all_to_all.29
  116.1 2.9 copy.11
  119.1 103.4 %all_to_all.36 = bf16[64,8,2048]{2,0,1:T(8,128)(2,1)} all-to-all(bf16[64,8,2048]{2,0,1:T(8,128)(2,1)S(1)} %copy.11), channel_id=1, replica_groups=mesh['row'=4,'col'=8] {'col'}, dimensions={1} | all-to-all | bytes 4194304 | tf_op jit(solution)/shard_map/all_to_all | solution.py:10
  222.4 0.0 all-gather.5.cloned.1.call-update
  222.5 0.0 copy-done.2
  222.5 0.0 copy-done.1
  222.5 0.0 copy-done
  222.5 0.1 exponential_multiply_fusion
  222.6 19.1 %all-gather.3.cloned.1.call-done = bf16[2048,4096]{1,0:T(8,128)(2,1)} async-done(((bf16[2048,512]{1,0:T(8,128)(2,1)}), bf16[2048,4096]{1,0:T(8,128)(2,1)}) %all-gather.3.cloned.1.call-update) | async-done | bytes 16777232 | tf_op jit(solution)/shard_map/all_gather | solution.py:13
  241.7 23.9 %copy.9 = f32[2048,4096]{0,1:T(8,128)} copy(bf16[2048,4096]{1,0:T(8,128)(2,1)} %all-gather.3.cloned.1.call-done) | data formatting | bytes 50331648 | tf_op jit(solution)/shard_map/convert_element_type | solution.py:13
  265.6 65.2 %all-gather.5.cloned.1.call-done = bf16[2048,2048]{1,0:T(8,128)(2,1)} async-done(((bf16[512,2048]{1,0:T(8,128)(2,1)}), bf16[2048,2048]{1,0:T(8,128)(2,1)}) %all-gather.5.cloned.1.call-update) | async-done | bytes 8388624 | tf_op jit(solution)/shard_map/all_gather | solution.py:11
  330.7 116.0 %fusion = f32[3,4096,2048]{2,1,0:T(8,128)} fusion(f32[3,2048]{1,0:T(4,128)S(1)} %exponential_multiply_fusion, f32[2048,4096]{0,1:T(8,128)} %copy.9, bf16[2048,2048]{1,0:T(8,128)(2,1)} %all-gather.5.cloned.1.call-done), kind=kOutput, calls=%fused_computation.1 | convolution fusion | flops 103129546752 | bytes 142630912 | tf_op jit(solution)/shard_map/trp,rq->tpq/dot_general | solution.py:16
  (1 shorter events, 0.0 us)
Async XLA Ops:
  6.5 215.9 %copy-start.2 = (f32[3]{0:T(128)S(1)}, f32[3]{0:T(128)}, u32[]{:S(2)}) copy-start(f32[3]{0:T(128)} %param.6) | copy-start | bytes 40
  6.5 216.0 %copy-start.1 = (f32[3]{0:T(128)S(1)}, f32[3]{0:T(128)}, u32[]{:S(2)}) copy-start(f32[3]{0:T(128)} %param.7) | copy-start | bytes 40
  6.5 216.0 %copy-start = (f32[2048]{0:T(1024)S(1)}, f32[2048]{0:T(1024)}, u32[]{:S(2)}) copy-start(f32[2048]{0:T(1024)} %param.5) | copy-start | bytes 24580
  6.5 235.2 %all-gather.3.cloned.1.call-start = ((), (), s32[]{:S(2)}) async-start(), calls=%async_computation.2 | async-start | bytes 18874368 | tf_op jit(solution)/shard_map/all_gather | solution.py:13
  7.3 323.5 %all-gather.5.cloned.1.call-start = ((), (), s32[]{:S(2)}) async-start(), calls=%async_computation.3 | async-start | bytes 10485760 | tf_op jit(solution)/shard_map/all_gather | solution.py:11
Sparse Core Ops, SparseCore 0:
  9.0 232.6 all-gather.2
  243.5 87.1 all-gather.4
where the time goes:
time: 457 us; the launch traced here: 454 us
  blocking collectives  208 us (46%)
  matrix products  116 us (25%)
  waiting for transfers between devices  85 us (19%)
  local copies, waits for them, and re-layouts  30.6 us (7%)
  between operations  13.4 us (3%)
    dot_general x1, matrix products, on_device(): jnp.einsum('trp,rq->tpq', weighted, col_whole, preferred_element_type=jnp...  116 us
    all_to_all x1, blocking collectives, on_device(): lax.all_to_all(pair_ints, ('row', 'col'), split_axis=0, concat_axis=1, ti...  105 us
    all_to_all x1, blocking collectives, on_device(): lax.all_to_all(pair_rows, 'col', split_axis=1, concat_axis=0, tiled=True)  103 us
    all_gather x1, waiting for transfers between devices, on_device(): col_whole = lax.all_gather(col_block, 'row', axis=0, tiled=True)  65.2 us
    convert_element_type x1, local copies, waits for them, and re-layouts, on_device(): lax.all_gather(pair_ints, 'col', axis=1, tiled=True).astype(jnp.float32)  23.9 us
    all_gather x1, waiting for transfers between devices, on_device(): lax.all_gather(pair_ints, 'col', axis=1, tiled=True).astype(jnp.float32)  19.1 us
  transfers between devices with their start and end apart: 2, of which 2 were waited for; matrix products, arithmetic and copies ran while one was open for 6% of the time, Pallas kernels for 0%

commit v1 on v0

v1 whole, which is shorter than its diff:
```python
import jax
import jax.numpy as jnp
from jax import lax
from jax.experimental import pallas as pl
from jax.experimental.pallas import tpu as pltpu
from jax.sharding import PartitionSpec as P

CHUNK = 512
SUB = 256
SLOTS = 3


def gemm_kernel(plan, offs_ref, fac_ref, *refs):
    n_rows, first, n_halves, groups, piece, hw, width, has_out, sub = plan
    refs = list(refs)
    row_refs = [refs.pop(0) for _ in range(n_rows)]
    col_refs = [[refs.pop(0) for _ in range(groups)] for _ in range(n_halves)]
    if has_out:
        refs.pop(0)
    out_ref = refs.pop(0)
    rows_v, cols_v, w_v, o_v, row_sem, col_sem, out_sem = refs
    nt, depth = fac_ref.shape
    kq = depth // groups
    per = CHUNK // hw
    per_half = groups // per
    chunks = n_halves * per_half
    subs = n_rows * piece // sub
    part = sub // chunks

    def row_copy(p):
        return pltpu.make_async_copy(row_refs[p], rows_v.at[pl.ds(p * piece, piece)], row_sem.at[p])

    def col_copies(h):
        out = []
        for g in range(groups):
            place = offs_ref[subs + g]
            for j in range(groups):
                i = lax.rem(place - j + groups, groups)
                c = h * per_half + i // per
                out.append(
                    pltpu.make_async_copy(
                        col_refs[h][g].at[j],
                        cols_v.at[c, pl.ds(pl.multiple_of(place * kq, kq), kq), pl.ds(pl.multiple_of(lax.rem(i, per) * hw, hw), hw)],
                        col_sem.at[h, g, j],
                    )
                )
        return out

    row_copy(0).start()
    for h in range(n_halves):
        for c in col_copies(h):
            c.start()
    for p in range(1, n_rows):
        row_copy(p).start()

    def weigh(slot, src, dst, count):
        x = rows_v[pl.ds(src, count), :].astype(jnp.float32)
        for t in range(nt):
            w_v[slot, pl.ds(t * sub + dst, count), :] = (x * fac_ref[pl.ds(t, 1), :]).astype(jnp.bfloat16)

    row_copy(0).wait()
    weigh(0, 0, 0, sub)
    for h in range(n_halves):
        for c in col_copies(h):
            c.wait()
    for p in range(1, n_rows):
        row_copy(p).wait()

    def out_copies(slot, s, n):
        h = n // per_half
        i0 = lax.rem(n, per_half) * per
        row0 = pl.multiple_of(offs_ref[s], sub)
        return [
            pltpu.make_async_copy(
                o_v.at[slot, :, :, pl.ds(e * hw, hw)],
                out_ref.at[:, pl.ds(row0, sub), pl.ds(pl.multiple_of((i0 + e) * width + (first + h) * hw, hw), hw)],
                out_sem.at[slot, e],
            )
            for e in range(per)
        ]

    total = subs * chunks

    def step(q, _):
        s, n = q // chunks, lax.rem(q, chunks)
        slot = lax.rem(q, SLOTS)
        cur = lax.rem(s, 2)

        @pl.when(q >= SLOTS)
        def _():
            for c in out_copies(slot, s, n):
                c.wait()

        nxt = jnp.minimum(s + 1, subs - 1)
        weigh(1 - cur, pl.multiple_of(nxt * sub + n * part, part), pl.multiple_of(n * part, part), part)
        res = jnp.dot(w_v[cur], cols_v[n], preferred_element_type=jnp.float32)
        o_v[slot] = res.reshape(nt, sub, CHUNK)
        for c in out_copies(slot, s, n):
            c.start()
        return 0

    lax.fori_loop(0, total, step, 0)
    for q in range(max(0, total - SLOTS), total):
        for c in out_copies(q % SLOTS, q // chunks, q % chunks):
            c.wait()


def gemm(factors, rows, row_offs, first, halves, places, out, out_shape, width):
    nt, depth = factors.shape
    piece = rows[0].shape[0]
    groups = len(halves[0])
    hw = halves[0][0].shape[2]
    sub = min(SUB, piece)
    offs = [o + k * sub for o in row_offs for k in range(piece // sub)] + list(places)
    offs = jnp.stack([jnp.asarray(o, jnp.int32) for o in offs])
    chunks = len(halves) * groups * hw // CHUNK
    plan = (len(rows), first, len(halves), groups, piece, hw, width, out is not None, sub)
    args = [factors, *rows, *[a for h in halves for a in h]]
    hbm = pl.BlockSpec(memory_space=pl.ANY)
    in_specs = [pl.BlockSpec(memory_space=pltpu.VMEM)] + [hbm] * (len(args) - 1)
    aliases = {}
    if out is not None:
        aliases = {len(args) + 1: 0}
        args.append(out)
        in_specs.append(hbm)
    m, n = len(rows) * piece, len(halves) * groups * hw
    return pl.pallas_call(
        lambda *refs: gemm_kernel(plan, *refs),
        out_shape=jax.ShapeDtypeStruct(out_shape, jnp.float32),
        grid_spec=pltpu.PrefetchScalarGridSpec(
            num_scalar_prefetch=1,
            grid=(),
            in_specs=in_specs,
            out_specs=hbm,
            scratch_shapes=[
                pltpu.VMEM((m, depth), jnp.bfloat16),
                pltpu.VMEM((chunks, depth, CHUNK), jnp.bfloat16),
                pltpu.VMEM((2, nt * sub, depth), jnp.bfloat16),
                pltpu.VMEM((SLOTS, nt, sub, CHUNK), jnp.float32),
                pltpu.SemaphoreType.DMA((len(rows),)),
                pltpu.SemaphoreType.DMA((len(halves), groups, groups)),
                pltpu.SemaphoreType.DMA((SLOTS, CHUNK // hw)),
            ],
        ),
        input_output_aliases=aliases,
        compiler_params=pltpu.CompilerParams(vmem_limit_bytes=48 * 1024 * 1024),
        cost_estimate=pl.CostEstimate(
            flops=2 * nt * m * n * depth,
            bytes_accessed=4 * nt * m * n + 2 * depth * (m + n),
            transcendentals=0,
        ),
    )(offs, *args)


def solution(mesh):
    R, C = mesh.shape["row"], mesh.shape["col"]
    Z = C // 2

    def on_device(pair_ints, denominators, lap_points, lap_weights):
        depth, width = pair_ints.shape
        r, u = lax.axis_index("row"), lax.axis_index("col")
        z, core = u // 2, lax.rem(u, 2)
        factors = lap_weights[:, None] * jnp.exp(-lap_points[:, None] * denominators[None, :])
        nt = factors.shape[0]
        kq = depth // R
        n_halves = 2 if width % 256 == 0 else 1
        hw = width // n_halves

        flat = r * C + u
        own = []
        for h in range(n_halves):
            pieces = []
            for j in range(R):
                q = lax.rem(lax.rem(flat, R) + j, R)
                piece = lax.dynamic_slice(pair_ints, (q * kq, h * hw), (kq, hw))
                perm = [(f, ((f % R + j) % R) * C + f // R) for f in range(R * C)]
                pieces.append(lax.ppermute(piece, ("row", "col"), perm))
            own.append(jnp.stack(pieces))

        def row_perm(x, e):
            return lax.ppermute(x, "row", [(a, a ^ e) for a in range(R)])

        halves = [[own[h]] + [row_perm(own[h], e) for e in range(1, R)] for h in range(n_halves)]
        places = [r ^ e for e in range(R)]

        def col_perm(x, pairs):
            return lax.ppermute(x, "col", [(2 * a + k, 2 * b + k) for a, b in pairs for k in range(2)])

        def swap(x):
            return lax.ppermute(x, "col", [(a, a ^ 1) for a in range(C)])

        mine = pair_ints.T
        arrivals = []
        if Z == 4:
            up = col_perm(mine, [((a + 1) % Z, a) for a in range(Z)])
            down = col_perm(mine, [((a - 1) % Z, a) for a in range(Z)])
            fwd = jnp.where(z == 1, up, jnp.where(z == 2, down, mine))
            pairs = [(1, 0), (2, 3), (3, 1), (0, 2)]
            m2 = width // 2
            arrivals = [
                (up, lax.rem(z + 1, Z), 0),
                (down, lax.rem(z + 3, Z), 0),
                (col_perm(fwd[:m2], pairs), lax.rem(z + 2, Z), 0),
                (col_perm(fwd[m2:], pairs), lax.rem(z + 2, Z), m2),
            ]
        else:
            for d in range(1, Z):
                arrivals.append((col_perm(mine, [((a + d) % Z, a) for a in range(Z)]), lax.rem(z + d, Z), 0))

        out_shape = (nt, C * width, R * width)

        def block(x, where, extra, first, hs, out):
            offs = [(2 * where + core) * width + extra, (2 * where + 1 - core) * width + extra]
            return gemm(factors, [x[0], x[1]], offs, first, hs, places, out, out_shape, width)

        pair = (mine, swap(mine))
        out = None
        for h in range(n_halves):
            out = block(pair, z, 0, h, [halves[h]], out)
        for x, where, extra in arrivals:
            out = block((x, swap(x)), where, extra, 0, halves, out)
        return out

    in_specs = (P(None, ("row", "col")), P(), P(), P())
    out_specs = P(None, "row", "col")
    return jax.shard_map(on_device, mesh=mesh, in_specs=in_specs, out_specs=out_specs, check_vma=False)
```

time: 457 us -> 461 us (level)
  blocking collectives: 208 us -> 0 us
  Pallas kernels: 0 us -> 158 us
  matrix products: 116 us -> 0 us
  waiting for transfers between devices: 85 us -> 190 us
  starting transfers between devices: 0.04 us -> 96.5 us
  local copies, waits for them, and re-layouts: 30.6 us -> 8.79 us
  between operations: 13.4 us -> 0.55 us
    all_to_all x2 -> x0, blocking collectives: 208 us -> none  [the longest x1 105 us: on_device(): lax.all_to_all(pair_ints, ('row', 'col'), split_axis=0, concat_axis=1, ti...]
    ppermute x0 -> x23, waiting for transfers between devices: none -> 190 us  [the longest x8 139 us: on_device(): pieces.append(lax.ppermute(piece, ('row', 'col'), perm))]
    pallas_call x0 -> x6, Pallas kernels: none -> 158 us  [gemm(): pl.pallas_call(lambda *refs: gemm_kernel(plan, *refs), out_shape=jax.Shap...]
    dot_general x1 -> x0, matrix products: 116 us -> none  [on_device(): jnp.einsum('trp,rq->tpq', weighted, col_whole, preferred_element_type=jnp...]
    ppermute x0 -> x23, starting transfers between devices: none -> 96.5 us  [the longest x8 77.4 us: on_device(): pieces.append(lax.ppermute(piece, ('row', 'col'), perm))]
    all_gather x2 -> x0, waiting for transfers between devices: 84.3 us -> none  [the longest x1 65.2 us: on_device(): col_whole = lax.all_gather(col_block, 'row', axis=0, tiled=True)]
    convert_element_type x1 -> x0, local copies, waits for them, and re-layouts: 23.9 us -> none  [on_device(): lax.all_gather(pair_ints, 'col', axis=1, tiled=True).astype(jnp.float32)]
    all_to_all x3 -> x0, local copies, waits for them, and re-layouts: 6.67 us -> none  [the longest x2 5.5 us: on_device(): lax.all_to_all(pair_rows, 'col', split_axis=1, concat_axis=0, tiled=True)]
  transfers between devices with their start and end apart: 2 -> 23, of which waited for: 2 -> 7; matrix products, arithmetic and copies ran while one was open for 6% -> 1% of each run, Pallas kernels for 0% -> 30%
where the time goes in v1:
time: 461 us; the launch traced here: 457 us
  waiting for transfers between devices  190 us (41%)
  Pallas kernels  158 us (34%)
  starting transfers between devices  96.5 us (21%)
  local copies, waits for them, and re-layouts  8.79 us (2%)
    pallas_call x6, Pallas kernels, gemm(): pl.pallas_call(lambda *refs: gemm_kernel(plan, *refs), out_shape=jax.Shap...  158 us
    ppermute x8, waiting for transfers between devices, on_device(): pieces.append(lax.ppermute(piece, ('row', 'col'), perm))  139 us
    ppermute x8, starting transfers between devices, on_device(): pieces.append(lax.ppermute(piece, ('row', 'col'), perm))  77.4 us
    ppermute x6, waiting for transfers between devices, row_perm(): return lax.ppermute(x, 'row', [(a, a ^ e) for a in range(R)])  50.8 us
    ppermute x6, starting transfers between devices, row_perm(): return lax.ppermute(x, 'row', [(a, a ^ e) for a in range(R)])  12.7 us
  transfers between devices with their start and end apart: 23, of which 7 were waited for; matrix products, arithmetic and copies ran while one was open for 1% of the time, Pallas kernels for 30%

profile of v1, /device:TPU:31, one launch (start us, length us, event | category | flops | bytes accessed | tf_op | source)
XLA Modules:
  0.0 457.0 jit_solution(12772141577304784825)
XLA Ops:
  0.0 2.9 copy.10
  3.2 3.1 collective-permute-start.1
  6.3 2.5 constant_dynamic-slice_fusion.3
  8.7 2.2 collective-permute-start.7
  10.9 0.7 collective-permute-start.4
  11.6 9.3 %collective-permute-start.5 = (bf16[512,256]{1,0:T(8,128)(2,1)S(1)}, bf16[512,256]{1,0:T(8,128)(2,1)S(1)}, u32[]{:S(2)}, u32[]{:S(2)}) collective-permute-start(bf16[512,256]{1,0:T(8,128)(2,1)S(1)} %get-tuple-element.11), channel_id=1, source_target_pairs={{0,8},{1,16},{2,24},{3,0},{4,9},{5,17},{6,25},{7,1},{8,10},{9,18},... | collective-permute-start | bytes 786440 | tf_op jit(solution)/shard_map/ppermute | solution.py:177
  20.9 129.4 %collective-permute-done.7 = bf16[512,256]{1,0:T(8,128)(2,1)S(1)} collective-permute-done((bf16[512,256]{1,0:T(8,128)(2,1)S(1)}, bf16[512,256]{1,0:T(8,128)(2,1)S(1)}, u32[]{:S(2)}, u32[]{:S(2)}) %collective-permute-start.7) | collective-permute-done | bytes 262176 | tf_op jit(solution)/shard_map/ppermute | solution.py:177
  150.3 0.7 collective-permute-start.11
  151.0 27.7 %collective-permute-start.12 = (bf16[512,256]{1,0:T(8,128)(2,1)S(1)}, bf16[512,256]{1,0:T(8,128)(2,1)S(1)}, u32[]{:S(2)}, u32[]{:S(2)}) collective-permute-start(bf16[512,256]{1,0:T(8,128)(2,1)S(1)} %get-tuple-element.8), channel_id=1, source_target_pairs={{0,8},{1,16},{2,24},{3,0},{4,9},{5,17},{6,25},{7,1},{8,10},{9,18},... | collective-permute-start | bytes 786440 | tf_op jit(solution)/shard_map/ppermute | solution.py:177
  178.7 2.5 collective-permute-done.6
  181.2 20.7 %collective-permute-start.13 = (bf16[512,256]{1,0:T(8,128)(2,1)}, bf16[512,256]{1,0:T(8,128)(2,1)}, u32[]{:S(2)}, u32[]{:S(2)}) collective-permute-start(bf16[512,256]{1,0:T(8,128)(2,1)} %get-tuple-element.14), channel_id=1, source_target_pairs={{0,16},{1,24},{2,0},{3,8},{4,17},{5,25},{6,1},{7,9},{8,18},{9,26},... | collective-permute-start | bytes 786440 | tf_op jit(solution)/shard_map/ppermute | solution.py:177
  201.9 16.2 %collective-permute-start.14 = (bf16[512,256]{1,0:T(8,128)(2,1)}, bf16[512,256]{1,0:T(8,128)(2,1)}, u32[]{:S(2)}, u32[]{:S(2)}) collective-permute-start(bf16[512,256]{1,0:T(8,128)(2,1)} %get-tuple-element.13), channel_id=1, source_target_pairs={{0,24},{1,0},{2,8},{3,16},{4,25},{5,1},{6,9},{7,17},{8,26},{9,2},{... | collective-permute-start | bytes 786440 | tf_op jit(solution)/shard_map/ppermute | solution.py:177
  218.8 1.1 pad_maximum_fusion.refs_4_
  220.5 3.4 collective-permute-start.10
  223.9 6.7 %collective-permute-done.14 = bf16[512,256]{1,0:T(8,128)(2,1)} collective-permute-done((bf16[512,256]{1,0:T(8,128)(2,1)}, bf16[512,256]{1,0:T(8,128)(2,1)}, u32[]{:S(2)}, u32[]{:S(2)}) %collective-permute-start.14) | collective-permute-done | bytes 262176 | tf_op jit(solution)/shard_map/ppermute | solution.py:177
  230.6 1.2 pad_maximum_fusion.1.refs_4_.refs_8_
  231.8 2.4 collective-permute-start.9
  234.2 1.5 collective-permute-start.15
  236.1 13.1 %collective-permute-done.10.refs_7_ = bf16[4,512,256]{2,1,0:T(8,128)(2,1)S(1)} collective-permute-done((bf16[4,512,256]{2,1,0:T(8,128)(2,1)S(1)}, bf16[4,512,256]{2,1,0:T(8,128)(2,1)S(1)}, u32[]{:S(2)}, u32[]{:S(2)}) %collective-permute-start.10) | collective-permute-done | bytes 1048608 | tf_op jit(solution)/shard_map/ppermute | solution.py:181
  249.2 2.5 collective-permute-start.16
  251.7 20.0 %collective-permute-done.8.refs_5_ = bf16[4,512,256]{2,1,0:T(8,128)(2,1)S(1)} collective-permute-done((bf16[4,512,256]{2,1,0:T(8,128)(2,1)S(1)}, bf16[4,512,256]{2,1,0:T(8,128)(2,1)S(1)}, u32[]{:S(2)}, u32[]{:S(2)}) %collective-permute-start.8) | collective-permute-done | bytes 1048608 | tf_op jit(solution)/shard_map/ppermute | solution.py:181
  271.7 3.0 collective-permute-start.17
  274.8 21.6 %shard_map.46.refs_8_ = f32[3,4096,2048]{2,1,0:T(8,128)} custom-call(s32[8]{0:T(128)S(1)} %stack.164.refs_0_, f32[3,2048]{1,0:T(4,128)S(1)} %exponential_multiply_fusion.refs_1_, bf16[512,2048]{1,0:T(8,128)(2,1)} %bitcast.33, bf16[512,2048]{1,0:T(8,128)(2,1)} %collective-permute-done.22.refs_3_, bf16[4,512,256]{2,1,0:T(8,128)(2,1)S(1)} %pad_maximum_fusion.refs_4_, ...), custom_call_target="tpu_custom_call" | custom-call | flops 12884901888 | bytes 20971520 | tf_op jit(solution)/shard_map/pallas_call | solution.py:127
  296.4 2.2 collective-permute-start.2
  298.9 17.8 %collective-permute-done.17.refs_7_.refs_11_ = bf16[4,512,256]{2,1,0:T(8,128)(2,1)S(1)} collective-permute-done((bf16[4,512,256]{2,1,0:T(8,128)(2,1)S(1)}, bf16[4,512,256]{2,1,0:T(8,128)(2,1)S(1)}, u32[]{:S(2)}, u32[]{:S(2)}) %collective-permute-start.17) | collective-permute-done | bytes 1048608 | tf_op jit(solution)/shard_map/ppermute | solution.py:181
  316.7 21.6 %shard_map.47.refs_12_ = f32[3,4096,2048]{2,1,0:T(8,128)} custom-call(s32[8]{0:T(128)S(1)} %stack.164.refs_0_, f32[3,2048]{1,0:T(4,128)S(1)} %exponential_multiply_fusion.refs_1_, bf16[512,2048]{1,0:T(8,128)(2,1)} %bitcast.34, bf16[512,2048]{1,0:T(8,128)(2,1)} %collective-permute-done.22.refs_3_, ...), custom_call_target="tpu_custom_call", output_to_operand_aliasing={{}: (8, {})} | custom-call | flops 12884901888 | bytes 20971520 | tf_op jit(solution)/shard_map/pallas_call | solution.py:127
  338.9 1.4 copy-done.6
  340.3 36.8 %shard_map.48.refs_12_ = f32[3,4096,2048]{2,1,0:T(8,128)} custom-call(s32[8]{0:T(128)S(1)} %stack.159.refs_0_, f32[3,2048]{1,0:T(4,128)S(1)} %exponential_multiply_fusion.refs_1_, bf16[512,2048]{1,0:T(8,128)(2,1)} %collective-permute-done.refs_2_, bf16[512,2048]{1,0:T(8,128)(2,1)} %copy-done.6, ...), custom_call_target="tpu_custom_call", output_to_operand_aliasing={{}: (12, {})} | custom-call | flops 25769803776 | bytes 37748736 | tf_op jit(solution)/shard_map/pallas_call | solution.py:127
  377.1 1.3 copy-done.7
  378.4 36.8 %shard_map.49.refs_12_ = f32[3,4096,2048]{2,1,0:T(8,128)} custom-call(s32[8]{0:T(128)S(1)} %stack.154.refs_0_, f32[3,2048]{1,0:T(4,128)S(1)} %exponential_multiply_fusion.refs_1_, bf16[512,2048]{1,0:T(8,128)(2,1)} %collective-permute-done.1.refs_2_, bf16[512,2048]{1,0:T(8,128)(2,1)} %copy-done.7, ...), custom_call_target="tpu_custom_call", output_to_operand_aliasing={{}: (12, {})} | custom-call | flops 25769803776 | bytes 37748736 | tf_op jit(solution)/shard_map/pallas_call | solution.py:127
  415.2 20.7 %shard_map.50.refs_12_ = f32[3,4096,2048]{2,1,0:T(8,128)} custom-call(s32[6]{0:T(128)S(1)} %stack.149.refs_0_, f32[3,2048]{1,0:T(4,128)S(1)} %exponential_multiply_fusion.refs_1_, bf16[256,2048]{1,0:T(8,128)(2,1)S(1)} %collective-permute-done.18.refs_2_, bf16[256,2048]{1,0:T(8,128)(2,1)S(1)} %collective-permute-done.19.refs_3_, ...), custom_call_target="tpu_custom_call", output_to_operand_aliasing={{}: (12, {})} | custom-call | flops 12884901888 | bytes 23068672 | tf_op jit(solution)/shard_map/pallas_call | solution.py:127
  435.9 20.9 %shard_map.51 = f32[3,4096,2048]{2,1,0:T(8,128)} custom-call(s32[6]{0:T(128)S(1)} %stack.136.refs_0_, f32[3,2048]{1,0:T(4,128)S(1)} %exponential_multiply_fusion.refs_1_, bf16[256,2048]{1,0:T(8,128)(2,1)} %collective-permute-done.2.refs_2_, bf16[256,2048]{1,0:T(8,128)(2,1)} %collective-permute-done.3.refs_3_, ...), custom_call_target="tpu_custom_call", output_to_operand_aliasing={{}: (12, {})} | custom-call | flops 12884901888 | bytes 23068672 | tf_op jit(solution)/shard_map/pallas_call | solution.py:127
  (55 shorter events, 2.9 us)
Async XLA Ops:
  2.9 232.7 %copy-start.5 = (bf16[2048,512]{0,1:T(8,128)(2,1)}, bf16[2048,512]{0,1:T(8,128)(2,1)S(1)}, u32[]{:S(2)}) copy-start(bf16[2048,512]{0,1:T(8,128)(2,1)S(1)} %copy.10) | copy-start | bytes 6291460
  2.9 228.8 %collective-permute-start = (bf16[512,2048]{1,0:T(8,128)(2,1)S(1)}, bf16[512,2048]{1,0:T(8,128)(2,1)}, u32[]{:S(2)}, u32[]{:S(2)}) collective-permute-start(bf16[512,2048]{1,0:T(8,128)(2,1)S(1)} %bitcast.30), channel_id=1, source_target_pairs={{2,0},{3,1},{4,2},{5,3},{6,4},{7,5},{0,6},{1,7},{10,8},{11,9},{12,... | collective-permute-start | bytes 6291464 | tf_op jit(solution)/shard_map/ppermute | solution.py:187
  3.2 231.0 %collective-permute-start.1 = (bf16[512,2048]{1,0:T(8,128)(2,1)S(1)}, bf16[512,2048]{1,0:T(8,128)(2,1)}, u32[]{:S(2)}, u32[]{:S(2)}) collective-permute-start(bf16[512,2048]{1,0:T(8,128)(2,1)S(1)} %bitcast.31), channel_id=1, source_target_pairs={{6,0},{7,1},{0,2},{1,3},{2,4},{3,5},{4,6},{5,7},{14,8},{15,9},{8,1... | collective-permute-start | bytes 6291464 | tf_op jit(solution)/shard_map/ppermute | solution.py:187
  6.3 174.9 %copy-start.10 = (f32[3]{0:T(128)S(1)}, f32[3]{0:T(128)}, u32[]{:S(2)}) copy-start(f32[3]{0:T(128)} %param.6) | copy-start | bytes 40
  6.3 211.9 %copy-start.8 = (f32[2048]{0:T(1024)S(1)}, f32[2048]{0:T(1024)}, u32[]{:S(2)}) copy-start(f32[2048]{0:T(1024)} %param.5) | copy-start | bytes 24580
  6.3 211.9 %copy-start.9 = (f32[3]{0:T(128)S(1)}, f32[3]{0:T(128)}, u32[]{:S(2)}) copy-start(f32[3]{0:T(128)} %param.7) | copy-start | bytes 40
  8.7 141.5 %collective-permute-start.7 = (bf16[512,256]{1,0:T(8,128)(2,1)S(1)}, bf16[512,256]{1,0:T(8,128)(2,1)S(1)}, u32[]{:S(2)}, u32[]{:S(2)}) collective-permute-start(bf16[512,256]{1,0:T(8,128)(2,1)S(1)} %get-tuple-element.9), channel_id=1, source_target_pairs={{0,24},{1,0},{2,8},{3,16},{4,25},{5,1},{6,9},{7,17},{8,26},{9,2},{... | collective-permute-start | bytes 786440 | tf_op jit(solution)/shard_map/ppermute | solution.py:177
  10.9 139.4 %collective-permute-start.4 = (bf16[512,256]{1,0:T(8,128)(2,1)S(1)}, bf16[512,256]{1,0:T(8,128)(2,1)S(1)}, u32[]{:S(2)}, u32[]{:S(2)}) collective-permute-start(bf16[512,256]{1,0:T(8,128)(2,1)S(1)} %get-tuple-element.12), channel_id=1, source_target_pairs={{0,0},{1,8},{2,16},{3,24},{4,1},{5,9},{6,17},{7,25},{8,2},{9,10},{... | collective-permute-start | bytes 786440 | tf_op jit(solution)/shard_map/ppermute | solution.py:177
  11.6 139.4 %collective-permute-start.5 = (bf16[512,256]{1,0:T(8,128)(2,1)S(1)}, bf16[512,256]{1,0:T(8,128)(2,1)S(1)}, u32[]{:S(2)}, u32[]{:S(2)}) collective-permute-start(bf16[512,256]{1,0:T(8,128)(2,1)S(1)} %get-tuple-element.11), channel_id=1, source_target_pairs={{0,8},{1,16},{2,24},{3,0},{4,9},{5,17},{6,25},{7,1},{8,10},{9,18},... | collective-permute-start | bytes 786440 | tf_op jit(solution)/shard_map/ppermute | solution.py:177
  150.3 30.9 %collective-permute-start.6 = (bf16[512,256]{1,0:T(8,128)(2,1)S(1)}, bf16[512,256]{1,0:T(8,128)(2,1)}, u32[]{:S(2)}, u32[]{:S(2)}) collective-permute-start(bf16[512,256]{1,0:T(8,128)(2,1)S(1)} %get-tuple-element.10), channel_id=1, source_target_pairs={{0,16},{1,24},{2,0},{3,8},{4,17},{5,25},{6,1},{7,9},{8,18},{9,26},... | collective-permute-start | bytes 786440 | tf_op jit(solution)/shard_map/ppermute | solution.py:177
  150.3 30.9 %collective-permute-start.11 = (bf16[512,256]{1,0:T(8,128)(2,1)S(1)}, bf16[512,256]{1,0:T(8,128)(2,1)S(1)}, u32[]{:S(2)}, u32[]{:S(2)}) collective-permute-start(bf16[512,256]{1,0:T(8,128)(2,1)S(1)} %get-tuple-element.7), channel_id=1, source_target_pairs={{0,0},{1,8},{2,16},{3,24},{4,1},{5,9},{6,17},{7,25},{8,2},{9,10},{... | collective-permute-start | bytes 786440 | tf_op jit(solution)/shard_map/ppermute | solution.py:177
  151.0 50.9 %collective-permute-start.12 = (bf16[512,256]{1,0:T(8,128)(2,1)S(1)}, bf16[512,256]{1,0:T(8,128)(2,1)S(1)}, u32[]{:S(2)}, u32[]{:S(2)}) collective-permute-start(bf16[512,256]{1,0:T(8,128)(2,1)S(1)} %get-tuple-element.8), channel_id=1, source_target_pairs={{0,8},{1,16},{2,24},{3,0},{4,9},{5,17},{6,25},{7,1},{8,10},{9,18},... | collective-permute-start | bytes 786440 | tf_op jit(solution)/shard_map/ppermute | solution.py:177
  181.2 93.5 %collective-permute-start.22 = (bf16[512,2048]{1,0:T(8,128)(2,1)S(1)}, bf16[512,2048]{1,0:T(8,128)(2,1)}, u32[]{:S(2)}, u32[]{:S(2)}) collective-permute-start(bf16[512,2048]{1,0:T(8,128)(2,1)S(1)} %bitcast.32), channel_id=1, source_target_pairs={{0,1},{1,0},{2,3},{3,2},{4,5},{5,4},{6,7},{7,6},{8,9},{9,8},{10,11... | collective-permute-start | bytes 6291464 | tf_op jit(solution)/shard_map/ppermute | solution.py:190
  181.2 39.3 %collective-permute-start.13 = (bf16[512,256]{1,0:T(8,128)(2,1)}, bf16[512,256]{1,0:T(8,128)(2,1)}, u32[]{:S(2)}, u32[]{:S(2)}) collective-permute-start(bf16[512,256]{1,0:T(8,128)(2,1)} %get-tuple-element.14), channel_id=1, source_target_pairs={{0,16},{1,24},{2,0},{3,8},{4,17},{5,25},{6,1},{7,9},{8,18},{9,26},... | collective-permute-start | bytes 786440 | tf_op jit(solution)/shard_map/ppermute | solution.py:177
  201.9 28.7 %collective-permute-start.14 = (bf16[512,256]{1,0:T(8,128)(2,1)}, bf16[512,256]{1,0:T(8,128)(2,1)}, u32[]{:S(2)}, u32[]{:S(2)}) collective-permute-start(bf16[512,256]{1,0:T(8,128)(2,1)} %get-tuple-element.13), channel_id=1, source_target_pairs={{0,24},{1,0},{2,8},{3,16},{4,25},{5,1},{6,9},{7,17},{8,26},{9,2},{... | collective-permute-start | bytes 786440 | tf_op jit(solution)/shard_map/ppermute | solution.py:177
  220.5 28.8 %collective-permute-start.10 = (bf16[4,512,256]{2,1,0:T(8,128)(2,1)S(1)}, bf16[4,512,256]{2,1,0:T(8,128)(2,1)S(1)}, u32[]{:S(2)}, u32[]{:S(2)}) collective-permute-start(bf16[4,512,256]{2,1,0:T(8,128)(2,1)S(1)} %pad_maximum_fusion.refs_4_), channel_id=1, source_target_pairs={{0,24},{8,16},{16,8},{24,0},{1,25},{9,17},{17,9},{25,1},{2,26},{10... | collective-permute-start | bytes 3145736 | tf_op jit(solution)/shard_map/ppermute | solution.py:181
  230.6 41.1 %collective-permute-start.8 = (bf16[4,512,256]{2,1,0:T(8,128)(2,1)S(1)}, bf16[4,512,256]{2,1,0:T(8,128)(2,1)S(1)}, u32[]{:S(2)}, u32[]{:S(2)}) collective-permute-start(bf16[4,512,256]{2,1,0:T(8,128)(2,1)S(1)} %pad_maximum_fusion.refs_4_), channel_id=1, source_target_pairs={{0,8},{8,0},{16,24},{24,16},{1,9},{9,1},{17,25},{25,17},{2,10},{10... | collective-permute-start | bytes 3145736 | tf_op jit(solution)/shard_map/ppermute | solution.py:181
  231.8 145.3 %copy-start = (bf16[4,512,256]{2,1,0:T(8,128)(2,1)}, bf16[4,512,256]{2,1,0:T(8,128)(2,1)S(1)}, u32[]{:S(2)}) copy-start(bf16[4,512,256]{2,1,0:T(8,128)(2,1)S(1)} %pad_maximum_fusion.1.refs_4_.refs_8_) | copy-start | bytes 3145732
  231.8 42.9 %collective-permute-start.9 = (bf16[4,512,256]{2,1,0:T(8,128)(2,1)S(1)}, bf16[4,512,256]{2,1,0:T(8,128)(2,1)S(1)}, u32[]{:S(2)}, u32[]{:S(2)}) collective-permute-start(bf16[4,512,256]{2,1,0:T(8,128)(2,1)S(1)} %pad_maximum_fusion.refs_4_), channel_id=1, source_target_pairs={{0,16},{8,24},{16,0},{24,8},{1,17},{9,25},{17,1},{25,9},{2,18},{10... | collective-permute-start | bytes 3145736 | tf_op jit(solution)/shard_map/ppermute | solution.py:181
  234.2 62.2 %collective-permute-start.15 = (bf16[4,512,256]{2,1,0:T(8,128)(2,1)S(1)}, bf16[4,512,256]{2,1,0:T(8,128)(2,1)S(1)}, u32[]{:S(2)}, u32[]{:S(2)}) collective-permute-start(bf16[4,512,256]{2,1,0:T(8,128)(2,1)S(1)} %pad_maximum_fusion.1.refs_4_.refs_8_), channel_id=1, source_target_pairs={{0,8},{8,0},{16,24},{24,16},{1,9},{9,1},{17,25},{25,17},{2,10},{10... | collective-permute-start | bytes 3145736 | tf_op jit(solution)/shard_map/ppermute | solution.py:181
  249.2 127.8 %copy-start.1 = (bf16[4,512,256]{2,1,0:T(8,128)(2,1)}, bf16[4,512,256]{2,1,0:T(8,128)(2,1)S(1)}, u32[]{:S(2)}) copy-start(bf16[4,512,256]{2,1,0:T(8,128)(2,1)S(1)} %collective-permute-done.10.refs_7_) | copy-start | bytes 3145732
  249.2 49.4 %collective-permute-start.16 = (bf16[4,512,256]{2,1,0:T(8,128)(2,1)S(1)}, bf16[4,512,256]{2,1,0:T(8,128)(2,1)S(1)}, u32[]{:S(2)}, u32[]{:S(2)}) collective-permute-start(bf16[4,512,256]{2,1,0:T(8,128)(2,1)S(1)} %pad_maximum_fusion.1.refs_4_.refs_8_), channel_id=1, source_target_pairs={{0,16},{8,24},{16,0},{24,8},{1,17},{9,25},{17,1},{25,9},{2,18},{10... | collective-permute-start | bytes 3145736 | tf_op jit(solution)/shard_map/ppermute | solution.py:181
  271.7 44.9 %collective-permute-start.17 = (bf16[4,512,256]{2,1,0:T(8,128)(2,1)S(1)}, bf16[4,512,256]{2,1,0:T(8,128)(2,1)S(1)}, u32[]{:S(2)}, u32[]{:S(2)}) collective-permute-start(bf16[4,512,256]{2,1,0:T(8,128)(2,1)S(1)} %pad_maximum_fusion.1.refs_4_.refs_8_), channel_id=1, source_target_pairs={{0,24},{8,16},{16,8},{24,0},{1,25},{9,17},{17,9},{25,1},{2,26},{10... | collective-permute-start | bytes 3145736 | tf_op jit(solution)/shard_map/ppermute | solution.py:181
  274.7 63.6 %collective-permute-start.18 = (bf16[256,2048]{1,0:T(8,128)(2,1)S(1)}, bf16[256,2048]{1,0:T(8,128)(2,1)S(1)}, u32[]{:S(2)}, u32[]{:S(2)}) collective-permute-start(bf16[256,2048]{1,0:T(8,128)(2,1)S(1)} %get-tuple-element.5), channel_id=1, source_target_pairs={{2,0},{3,1},{4,6},{5,7},{6,2},{7,3},{0,4},{1,5},{10,8},{11,9},{12,... | collective-permute-start | bytes 3145736 | tf_op jit(solution)/shard_map/ppermute | solution.py:187
  274.7 64.2 %collective-permute-start.21 = (bf16[512,2048]{1,0:T(8,128)(2,1)}, bf16[512,2048]{1,0:T(8,128)(2,1)S(1)}, u32[]{:S(2)}, u32[]{:S(2)}) collective-permute-start(bf16[512,2048]{1,0:T(8,128)(2,1)} %collective-permute-done.refs_2_), channel_id=1, source_target_pairs={{0,1},{1,0},{2,3},{3,2},{4,5},{5,4},{6,7},{7,6},{8,9},{9,8},{10,11... | collective-permute-start | bytes 6291464 | tf_op jit(solution)/shard_map/ppermute | solution.py:190
  296.4 41.9 %copy-start.2 = (bf16[4,512,256]{2,1,0:T(8,128)(2,1)}, bf16[4,512,256]{2,1,0:T(8,128)(2,1)S(1)}, u32[]{:S(2)}) copy-start(bf16[4,512,256]{2,1,0:T(8,128)(2,1)S(1)} %collective-permute-done.15.refs_5_.refs_9_) | copy-start | bytes 3145732
  296.4 42.4 %collective-permute-start.2 = (bf16[256,2048]{1,0:T(8,128)(2,1)S(1)}, bf16[256,2048]{1,0:T(8,128)(2,1)}, u32[]{:S(2)}, u32[]{:S(2)}) collective-permute-start(bf16[256,2048]{1,0:T(8,128)(2,1)S(1)} %get-tuple-element.6), channel_id=1, source_target_pairs={{2,0},{3,1},{4,6},{5,7},{6,2},{7,3},{0,4},{1,5},{10,8},{11,9},{12,... | collective-permute-start | bytes 3145736 | tf_op jit(solution)/shard_map/ppermute | solution.py:187
  298.6 39.7 %copy-start.3 = (bf16[4,512,256]{2,1,0:T(8,128)(2,1)}, bf16[4,512,256]{2,1,0:T(8,128)(2,1)S(1)}, u32[]{:S(2)}) copy-start(bf16[4,512,256]{2,1,0:T(8,128)(2,1)S(1)} %collective-permute-done.16.refs_6_.refs_10_) | copy-start | bytes 3145732
  298.6 78.4 %collective-permute-start.20 = (bf16[512,2048]{1,0:T(8,128)(2,1)}, bf16[512,2048]{1,0:T(8,128)(2,1)S(1)}, u32[]{:S(2)}, u32[]{:S(2)}) collective-permute-start(bf16[512,2048]{1,0:T(8,128)(2,1)} %collective-permute-done.1.refs_2_), channel_id=1, source_target_pairs={{0,1},{1,0},{2,3},{3,2},{4,5},{5,4},{6,7},{7,6},{8,9},{9,8},{10,11... | collective-permute-start | bytes 6291464 | tf_op jit(solution)/shard_map/ppermute | solution.py:190
  316.7 21.6 %copy-start.4 = (bf16[4,512,256]{2,1,0:T(8,128)(2,1)}, bf16[4,512,256]{2,1,0:T(8,128)(2,1)S(1)}, u32[]{:S(2)}) copy-start(bf16[4,512,256]{2,1,0:T(8,128)(2,1)S(1)} %collective-permute-done.17.refs_7_.refs_11_) | copy-start | bytes 3145732
  338.3 76.9 %collective-permute-start.19 = (bf16[256,2048]{1,0:T(8,128)(2,1)S(1)}, bf16[256,2048]{1,0:T(8,128)(2,1)S(1)}, u32[]{:S(2)}, u32[]{:S(2)}) collective-permute-start(bf16[256,2048]{1,0:T(8,128)(2,1)S(1)} %collective-permute-done.18.refs_2_), channel_id=1, source_target_pairs={{0,1},{1,0},{2,3},{3,2},{4,5},{5,4},{6,7},{7,6},{8,9},{9,8},{10,11... | collective-permute-start | bytes 3145736 | tf_op jit(solution)/shard_map/ppermute | solution.py:190
  338.8 97.1 %collective-permute-start.3 = (bf16[256,2048]{1,0:T(8,128)(2,1)}, bf16[256,2048]{1,0:T(8,128)(2,1)}, u32[]{:S(2)}, u32[]{:S(2)}) collective-permute-start(bf16[256,2048]{1,0:T(8,128)(2,1)} %collective-permute-done.2.refs_2_), channel_id=1, source_target_pairs={{0,1},{1,0},{2,3},{3,2},{4,5},{5,4},{6,7},{7,6},{8,9},{9,8},{10,11... | collective-permute-start | bytes 3145736 | tf_op jit(solution)/shard_map/ppermute | solution.py:190
  (2 other events, 2.7 us)

commit v2 on v1

v2 whole, which is shorter than its diff:
```python
import jax
import jax.numpy as jnp
from jax import lax
from jax.experimental import pallas as pl
from jax.experimental.pallas import tpu as pltpu
from jax.sharding import PartitionSpec as P

CHUNK = 512
SUB = 512
SLOTS = 3
COST = 2


def gemm_kernel(plan, offs_ref, fac_ref, *refs):
    n_rows, first, n_halves, groups, piece, hw, width, n_more, sub = plan
    refs = list(refs)
    row_refs = [refs.pop(0) for _ in range(n_rows)]
    col_refs = [[refs.pop(0) for _ in range(groups)] for _ in range(n_halves)]
    refs = refs[n_more:]
    out_ref, tok_ref = refs.pop(0), refs.pop(0)
    tok_ref[...] = jnp.zeros_like(tok_ref)
    rows_v, cols_v, w_v, o_v, row_sem, col_sem, out_sem = refs
    nt, depth = fac_ref.shape
    per = CHUNK // hw
    per_half = groups // per
    chunks = n_halves * per_half
    subs = n_rows * piece // sub
    part = sub // chunks

    def row_copy(p):
        return pltpu.make_async_copy(row_refs[p], rows_v.at[pl.ds(p * piece, piece)], row_sem.at[p])

    def col_copy(h, g, sem_h, sem_g):
        i = offs_ref[subs + g]
        return pltpu.make_async_copy(
            col_refs[h][g],
            cols_v.at[h * per_half + i // per, :, pl.ds(pl.multiple_of(lax.rem(i, per) * hw, hw), hw)],
            col_sem.at[sem_h, sem_g],
        )

    row_copy(0).start()
    for h in range(n_halves):
        for g in range(groups):
            col_copy(h, g, h, g).start()
    for p in range(1, n_rows):
        row_copy(p).start()

    def weigh(slot, src, dst, count):
        x = rows_v[pl.ds(src, count), :].astype(jnp.float32)
        for t in range(nt):
            w_v[slot, pl.ds(t * sub + dst, count), :] = (x * fac_ref[pl.ds(t, 1), :]).astype(jnp.bfloat16)

    row_copy(0).wait()
    weigh(0, 0, 0, sub)

    def out_copies(slot, s, n):
        h = n // per_half
        i0 = lax.rem(n, per_half) * per
        row0 = pl.multiple_of(offs_ref[s], sub)
        return [
            pltpu.make_async_copy(
                o_v.at[slot, :, :, pl.ds(e * hw, hw)],
                out_ref.at[:, pl.ds(row0, sub), pl.ds(pl.multiple_of((i0 + e) * width + (first + h) * hw, hw), hw)],
                out_sem.at[slot, e],
            )
            for e in range(per)
        ]

    total = subs * chunks

    def step(q, _):
        s, n = q // chunks, lax.rem(q, chunks)
        slot = lax.rem(q, SLOTS)
        cur = lax.rem(s, 2)

        @pl.when(s == 0)
        def _():
            h = n // per_half
            for e in range(per):
                g = offs_ref[subs + lax.rem(n, per_half) * per + e]
                col_copy(0, 0, h, g).wait()

        for p in range(1, n_rows):

            @pl.when((n == 0) & (s + 1 == p * (piece // sub)))
            def _():
                row_copy(p).wait()

        @pl.when(q >= SLOTS)
        def _():
            for c in out_copies(slot, s, n):
                c.wait()

        nxt = jnp.minimum(s + 1, subs - 1)
        weigh(1 - cur, pl.multiple_of(nxt * sub + n * part, part), pl.multiple_of(n * part, part), part)
        res = jnp.dot(w_v[cur], cols_v[n], preferred_element_type=jnp.float32)
        o_v[slot] = res.reshape(nt, sub, CHUNK)
        for c in out_copies(slot, s, n):
            c.start()
        return 0

    lax.fori_loop(0, total, step, 0)
    for q in range(max(0, total - SLOTS), total):
        for c in out_copies(q % SLOTS, q // chunks, q % chunks):
            c.wait()


def tie(x, *deps):
    hbm = pl.BlockSpec(memory_space=pl.ANY)
    return pl.pallas_call(
        lambda *refs: None,
        out_shape=jax.ShapeDtypeStruct(x.shape, x.dtype),
        in_specs=[hbm] * (1 + len(deps)),
        out_specs=hbm,
        input_output_aliases={0: 0},
        compiler_params=pltpu.CompilerParams(vmem_limit_bytes=48 * 1024 * 1024),
    )(x, *deps)


def gemm(factors, rows, row_offs, first, halves, places, out, out_shape, width, deps=()):
    nt, depth = factors.shape
    piece = rows[0].shape[0]
    groups = len(halves[0])
    hw = halves[0][0].shape[1]
    sub = min(SUB, piece)
    offs = [o + k * sub for o in row_offs for k in range(piece // sub)] + list(places)
    offs = jnp.stack([jnp.asarray(o, jnp.int32) for o in offs])
    chunks = len(halves) * groups * hw // CHUNK
    plan = (len(rows), first, len(halves), groups, piece, hw, width, len(deps) + (out is not None), sub)
    args = [factors, *rows, *[a for h in halves for a in h], *deps]
    hbm = pl.BlockSpec(memory_space=pl.ANY)
    in_specs = [pl.BlockSpec(memory_space=pltpu.VMEM)] + [hbm] * (len(args) - 1)
    aliases = {}
    if out is not None:
        aliases = {len(args) + 1: 0}
        args.append(out)
        in_specs.append(hbm)
    m, n = len(rows) * piece, len(halves) * groups * hw
    return pl.pallas_call(
        lambda *refs: gemm_kernel(plan, *refs),
        out_shape=(jax.ShapeDtypeStruct(out_shape, jnp.float32), jax.ShapeDtypeStruct((8, 128), jnp.float32)),
        grid_spec=pltpu.PrefetchScalarGridSpec(
            num_scalar_prefetch=1,
            grid=(),
            in_specs=in_specs,
            out_specs=(hbm, pl.BlockSpec(memory_space=pltpu.VMEM)),
            scratch_shapes=[
                pltpu.VMEM((m, depth), jnp.bfloat16),
                pltpu.VMEM((chunks, depth, CHUNK), jnp.bfloat16),
                pltpu.VMEM((2, nt * sub, depth), jnp.bfloat16),
                pltpu.VMEM((SLOTS, nt, sub, CHUNK), jnp.float32),
                pltpu.SemaphoreType.DMA((len(rows),)),
                pltpu.SemaphoreType.DMA((len(halves), groups)),
                pltpu.SemaphoreType.DMA((SLOTS, CHUNK // hw)),
            ],
        ),
        input_output_aliases=aliases,
        compiler_params=pltpu.CompilerParams(vmem_limit_bytes=48 * 1024 * 1024),
        cost_estimate=pl.CostEstimate(
            flops=COST * nt * m * n * depth,
            bytes_accessed=4 * nt * m * n + 2 * depth * (m + n),
            transcendentals=0,
        ),
    )(offs, *args)


def solution(mesh):
    R, C = mesh.shape["row"], mesh.shape["col"]
    Z = C // 2

    def on_device(pair_ints, denominators, lap_points, lap_weights):
        depth, width = pair_ints.shape
        r, u = lax.axis_index("row"), lax.axis_index("col")
        z, core = u // 2, lax.rem(u, 2)
        factors = lap_weights[:, None] * jnp.exp(-lap_points[:, None] * denominators[None, :])
        nt = factors.shape[0]
        n_halves = 2 if width % 256 == 0 else 1
        hw = width // n_halves

        perm = [(f, (f % R) * C + f // R) for f in range(R * C)]
        own = [lax.ppermute(pair_ints[:, h * hw : (h + 1) * hw], ("row", "col"), perm) for h in range(n_halves)]

        def row_perm(x, e):
            return lax.ppermute(x, "row", [(a, a ^ e) for a in range(R)])

        halves = [[own[h]] + [row_perm(own[h], e) for e in range(1, R)] for h in range(n_halves)]
        places = [r ^ e for e in range(R)]

        def col_perm(x, pairs):
            return lax.ppermute(x, "col", [(2 * a + k, 2 * b + k) for a, b in pairs for k in range(2)])

        def swap(x):
            return lax.ppermute(x, "col", [(a, a ^ 1) for a in range(C)])

        out_shape = (nt, C * width, R * width)

        def block(x, where, extra, first, hs, out, deps=()):
            offs = [(2 * where + core) * width + extra, (2 * where + 1 - core) * width + extra]
            return gemm(factors, [x[0], x[1]], offs, first, hs, places, out, out_shape, width, deps)

        mine = pair_ints.T
        late = tie(mine, *own)
        out = None
        for h in range(n_halves):
            out, token = block((mine, swap(mine)), z, 0, h, [halves[h]], out, (late,))
        if Z != 4:
            for d in range(1, Z):
                x = col_perm(late, [((a + d) % Z, a) for a in range(Z)])
                out, _ = block((x, swap(x)), lax.rem(z + d, Z), 0, 0, halves, out)
            return out

        up = col_perm(late, [((a + 1) % Z, a) for a in range(Z)])
        down = col_perm(late, [((a - 1) % Z, a) for a in range(Z)])
        fwd = tie(jnp.where(z == 1, up, jnp.where(z == 2, down, late)), token)
        pairs = [(1, 0), (2, 3), (3, 1), (0, 2)]
        m2 = width // 2
        last = [col_perm(fwd[:m2], pairs), col_perm(fwd[m2:], pairs)]
        tokens = []
        for x, d in ((up, 1), (down, Z - 1)):
            out, token = block((x, swap(x)), lax.rem(z + d, Z), 0, 0, halves, out)
            tokens.append(token)
        for k in range(2):
            x = tie(last[k], tokens[k])
            out, _ = block((x, swap(x)), lax.rem(z + 2, Z), k * m2, 0, halves, out)
        return out

    in_specs = (P(None, ("row", "col")), P(), P(), P())
    out_specs = P(None, "row", "col")
    return jax.shard_map(on_device, mesh=mesh, in_specs=in_specs, out_specs=out_specs, check_vma=False)
```

time: 461 us -> 397 us (0.86)
  waiting for transfers between devices: 190 us -> 29.1 us
  starting transfers between devices: 96.5 us -> 196 us
    ppermute x8 -> x2, waiting for transfers between devices: 139 us -> 0.01 us  [on_device(): lax.ppermute(pair_ints[:, h * hw:(h + 1) * hw], ('row', 'col'), perm)]
    ppermute x6, starting transfers between devices: 12.7 us -> 120 us  [row_perm(): return lax.ppermute(x, 'row', [(a, a ^ e) for a in range(R)])]
    ppermute x8 -> x2, starting transfers between devices: 77.4 us -> 3.53 us  [on_device(): lax.ppermute(pair_ints[:, h * hw:(h + 1) * hw], ('row', 'col'), perm)]
    ppermute x4, starting transfers between devices: 5.53 us -> 61.8 us  [col_perm(): lax.ppermute(x, 'col', [(2 * a + k, 2 * b + k) for a, b in pairs for k in...]
    ppermute x6, waiting for transfers between devices: 50.8 us -> 2.8 us  [row_perm(): return lax.ppermute(x, 'row', [(a, a ^ e) for a in range(R)])]
    ppermute x4, waiting for transfers between devices: 0.01 us -> 26.3 us  [col_perm(): lax.ppermute(x, 'col', [(2 * a + k, 2 * b + k) for a, b in pairs for k in...]
    ppermute x5, starting transfers between devices: 0.94 us -> 10.5 us  [swap(): return lax.ppermute(x, 'col', [(a, a ^ 1) for a in range(C)])]
    pallas_call x6 -> x10, Pallas kernels: 158 us -> 160 us  [the longest x6 160 us: gemm(): pl.pallas_call(lambda *refs: gemm_kernel(plan, *refs), out_shape=(jax.Sha...]
  transfers between devices with their start and end apart: 23 -> 17, of which waited for: 7 -> 3; matrix products, arithmetic and copies ran while one was open for 1% -> 1% of each run, Pallas kernels for 30% -> 35%
where the time goes in v2:
time: 397 us; the launch traced here: 396 us
  starting transfers between devices  196 us (49%)
  Pallas kernels  160 us (40%)
  waiting for transfers between devices  29.1 us (7%)
  local copies, waits for them, and re-layouts  10.2 us (3%)
    pallas_call x6, Pallas kernels, gemm(): pl.pallas_call(lambda *refs: gemm_kernel(plan, *refs), out_shape=(jax.Sha...  160 us
    ppermute x6, starting transfers between devices, row_perm(): return lax.ppermute(x, 'row', [(a, a ^ e) for a in range(R)])  120 us
    ppermute x4, starting transfers between devices, col_perm(): lax.ppermute(x, 'col', [(2 * a + k, 2 * b + k) for a, b in pairs for k in...  61.8 us
    ppermute x4, waiting for transfers between devices, col_perm(): lax.ppermute(x, 'col', [(2 * a + k, 2 * b + k) for a, b in pairs for k in...  26.3 us
    ppermute x5, starting transfers between devices, swap(): return lax.ppermute(x, 'col', [(a, a ^ 1) for a in range(C)])  10.5 us
  transfers between devices with their start and end apart: 17, of which 3 were waited for; matrix products, arithmetic and copies ran while one was open for 1% of the time, Pallas kernels for 35%

profile of v2, /device:TPU:31, one launch (start us, length us, event | category | flops | bytes accessed | tf_op | source)
XLA Modules:
  0.0 396.4 jit_solution(14422393614330427396)
XLA Ops:
  0.0 2.8 fusion.1
  2.8 1.7 collective-permute-start
  4.5 2.5 copy.14
  6.9 1.0 collective-permute-start.4
  7.9 1.9 collective-permute-start.1
  9.7 112.3 %collective-permute-start.10 = (bf16[2048,256]{1,0:T(8,128)(2,1)}, bf16[2048,256]{1,0:T(8,128)(2,1)}, u32[]{:S(2)}, u32[]{:S(2)}) collective-permute-start(bf16[2048,256]{1,0:T(8,128)(2,1)} %collective-permute-done.refs_1_.refs_4_), channel_id=1, source_target_pairs={{0,24},{8,16},{16,8},{24,0},{1,25},{9,17},{17,9},{25,1},{2,26},{10... | collective-permute-start | bytes 3145736 | tf_op jit(solution)/shard_map/ppermute | solution.py:184
  122.1 0.3 collective-permute-start.9
  122.3 1.6 copy.15.refs_0_
  124.0 57.5 %collective-permute-start.2 = (bf16[512,2048]{1,0:T(8,128)(2,1)S(1)}, bf16[512,2048]{1,0:T(8,128)(2,1)}, u32[]{:S(2)}, u32[]{:S(2)}) collective-permute-start(bf16[512,2048]{1,0:T(8,128)(2,1)S(1)} %shard_map.46.refs_8_), channel_id=1, source_target_pairs={{2,0},{3,1},{4,2},{5,3},{6,4},{7,5},{0,6},{1,7},{10,8},{11,9},{12,... | collective-permute-start | bytes 6291464 | tf_op jit(solution)/shard_map/ppermute | solution.py:190
  181.4 0.1 stack.89.refs_0_
  181.5 0.1 stack.95.refs_0_
  181.6 0.1 stack.92.refs_0_
  181.8 0.1 stack.86.refs_0_
  181.9 0.1 exponential_multiply_fusion.refs_1_
  182.1 7.3 %collective-permute-start.6 = (bf16[2048,256]{1,0:T(8,128)(2,1)S(1)}, bf16[2048,256]{1,0:T(8,128)(2,1)S(1)}, u32[]{:S(2)}, u32[]{:S(2)}) collective-permute-start(bf16[2048,256]{1,0:T(8,128)(2,1)S(1)} %collective-permute-done.1.refs_2_.refs_4_.refs_8_), channel_id=1, source_target_pairs={{0,16},{8,24},{16,0},{24,8},{1,17},{9,25},{17,1},{25,9},{2,18},{10... | collective-permute-start | bytes 3145736 | tf_op jit(solution)/shard_map/ppermute | solution.py:184
  189.5 23.4 %shard_map.47 = (f32[3,4096,2048]{2,1,0:T(8,128)}, f32[8,128]{1,0:T(8,128)}) custom-call(s32[6]{0:T(128)S(1)} %stack.89.refs_0_, f32[3,2048]{1,0:T(4,128)S(1)} %exponential_multiply_fusion.refs_1_, bf16[512,2048]{1,0:T(8,128)(2,1)} %bitcast.6.refs_2_, bf16[512,2048]{1,0:T(8,128)(2,1)} %collective-permute-done.4.refs_3_, ...), custom_call_target="tpu_custom_call" | custom-call | flops 12884901888 | bytes 20971520 | tf_op jit(solution)/shard_map/pallas_call | solution.py:139
  212.9 11.8 %collective-permute-done.2.refs_2_ = bf16[512,2048]{1,0:T(8,128)(2,1)} collective-permute-done((bf16[512,2048]{1,0:T(8,128)(2,1)S(1)}, bf16[512,2048]{1,0:T(8,128)(2,1)}, u32[]{:S(2)}, u32[]{:S(2)}) %collective-permute-start.2) | collective-permute-done | bytes 2097184 | tf_op jit(solution)/shard_map/ppermute | solution.py:190
  224.7 4.9 %collective-permute-start.13 = (bf16[512,2048]{1,0:T(8,128)(2,1)}, bf16[512,2048]{1,0:T(8,128)(2,1)S(1)}, u32[]{:S(2)}, u32[]{:S(2)}) collective-permute-start(bf16[512,2048]{1,0:T(8,128)(2,1)} %collective-permute-done.2.refs_2_), channel_id=1, source_target_pairs={{0,1},{1,0},{2,3},{3,2},{4,5},{5,4},{6,7},{7,6},{8,9},{9,8},{10,11... | collective-permute-start | bytes 6291464 | tf_op jit(solution)/shard_map/ppermute | solution.py:193
  229.5 2.8 collective-permute-done.6.refs_6_.refs_10_
  232.3 22.7 %shard_map.48 = (f32[3,4096,2048]{2,1,0:T(8,128)}, f32[8,128]{1,0:T(8,128)S(1)}) custom-call(s32[6]{0:T(128)S(1)} %stack.89.refs_0_, f32[3,2048]{1,0:T(4,128)S(1)} %exponential_multiply_fusion.refs_1_, bf16[512,2048]{1,0:T(8,128)(2,1)} %bitcast.6.refs_2_, bf16[512,2048]{1,0:T(8,128)(2,1)} %collective-permute-done.4.refs_3_, ...), custom_call_target="tpu_custom_call", output_to_operand_aliasing={{0}: (9, {})} | custom-call | flops 12884901888 | bytes 20971520 | tf_op jit(solution)/shard_map/pallas_call | solution.py:139
  255.1 14.5 %collective-permute-done.3.refs_2_ = bf16[512,2048]{1,0:T(8,128)(2,1)S(1)} collective-permute-done((bf16[512,2048]{1,0:T(8,128)(2,1)S(1)}, bf16[512,2048]{1,0:T(8,128)(2,1)S(1)}, u32[]{:S(2)}, u32[]{:S(2)}) %collective-permute-start.3) | collective-permute-done | bytes 2097184 | tf_op jit(solution)/shard_map/ppermute | solution.py:190
  269.6 0.5 select_select_fusion.refs_0_
  270.1 0.2 fusion
  270.5 4.3 %collective-permute-start.11 = (bf16[256,2048]{1,0:T(8,128)(2,1)S(1)}, bf16[256,2048]{1,0:T(8,128)(2,1)S(1)}, u32[]{:S(2)}, u32[]{:S(2)}) collective-permute-start(bf16[256,2048]{1,0:T(8,128)(2,1)S(1)} %get-tuple-element.24), channel_id=1, source_target_pairs={{2,0},{3,1},{4,6},{5,7},{6,2},{7,3},{0,4},{1,5},{10,8},{11,9},{12,... | collective-permute-start | bytes 3145736 | tf_op jit(solution)/shard_map/ppermute | solution.py:190
  274.7 4.0 %collective-permute-start.12 = (bf16[512,2048]{1,0:T(8,128)(2,1)S(1)}, bf16[512,2048]{1,0:T(8,128)(2,1)S(1)}, u32[]{:S(2)}, u32[]{:S(2)}) collective-permute-start(bf16[512,2048]{1,0:T(8,128)(2,1)S(1)} %collective-permute-done.3.refs_2_), channel_id=1, source_target_pairs={{0,1},{1,0},{2,3},{3,2},{4,5},{5,4},{6,7},{7,6},{8,9},{9,8},{10,11... | collective-permute-start | bytes 6291464 | tf_op jit(solution)/shard_map/ppermute | solution.py:193
  278.7 1.3 copy-done.8
  280.1 36.6 %shard_map.50 = (f32[3,4096,2048]{2,1,0:T(8,128)}, f32[8,128]{1,0:T(8,128)S(1)}) custom-call(s32[6]{0:T(128)S(1)} %stack.95.refs_0_, f32[3,2048]{1,0:T(4,128)S(1)} %exponential_multiply_fusion.refs_1_, bf16[512,2048]{1,0:T(8,128)(2,1)} %collective-permute-done.2.refs_2_, bf16[512,2048]{1,0:T(8,128)(2,1)} %copy-done.8, ...), custom_call_target="tpu_custom_call", output_to_operand_aliasing={{0}: (12, {})} | custom-call | flops 25769803776 | bytes 37748736 | tf_op jit(solution)/shard_map/pallas_call | solution.py:139
  316.8 1.3 copy-done.9
  318.1 36.6 %shard_map.51 = (f32[3,4096,2048]{2,1,0:T(8,128)}, f32[8,128]{1,0:T(8,128)S(1)}) custom-call(s32[6]{0:T(128)S(1)} %stack.92.refs_0_, f32[3,2048]{1,0:T(4,128)S(1)} %exponential_multiply_fusion.refs_1_, bf16[512,2048]{1,0:T(8,128)(2,1)} %copy-done.7, bf16[512,2048]{1,0:T(8,128)(2,1)} %copy-done.9, ...), custom_call_target="tpu_custom_call", output_to_operand_aliasing={{0}: (12, {})} | custom-call | flops 25769803776 | bytes 37748736 | tf_op jit(solution)/shard_map/pallas_call | solution.py:139
  354.7 0.6 collective-permute-start.14
  355.3 20.5 %shard_map.54 = (f32[3,4096,2048]{2,1,0:T(8,128)}, f32[8,128]{1,0:T(8,128)}) custom-call(s32[6]{0:T(128)S(1)} %stack.98.refs_0_, f32[3,2048]{1,0:T(4,128)S(1)} %exponential_multiply_fusion.refs_1_, bf16[256,2048]{1,0:T(8,128)(2,1)S(1)} %shard_map.53.refs_2_, bf16[256,2048]{1,0:T(8,128)(2,1)S(1)} %collective-permute-done.16.refs_3_, ...), custom_call_target="tpu_custom_call", output_to_operand_aliasing={{0}: (12, {})} | custom-call | flops 12884901888 | bytes 23068672 | tf_op jit(solution)/shard_map/pallas_call | solution.py:139
  375.8 20.5 %shard_map.55 = (f32[3,4096,2048]{2,1,0:T(8,128)}, f32[8,128]{1,0:T(8,128)}) custom-call(s32[6]{0:T(128)S(1)} %stack.86.refs_0_, f32[3,2048]{1,0:T(4,128)S(1)} %exponential_multiply_fusion.refs_1_, bf16[256,2048]{1,0:T(8,128)(2,1)S(1)} %shard_map.52.refs_2_, bf16[256,2048]{1,0:T(8,128)(2,1)S(1)} %collective-permute-done.14.refs_3_, ...), custom_call_target="tpu_custom_call", output_to_operand_aliasing={{0}: (12, {})} | custom-call | flops 12884901888 | bytes 23068672 | tf_op jit(solution)/shard_map/pallas_call | solution.py:139
  (50 shorter events, 0.4 us)
Async XLA Ops:
  0.0 4.5 %copy-start.6 = (bf16[2048,512]{1,0:T(8,128)(2,1)S(1)}, bf16[2048,512]{1,0:T(8,128)(2,1)}, u32[]{:S(2)}) copy-start(bf16[2048,512]{1,0:T(8,128)(2,1)} %param.4) | copy-start | bytes 6291460
  2.8 6.9 %collective-permute-start = (bf16[2048,256]{1,0:T(8,128)(2,1)S(1)}, bf16[2048,256]{1,0:T(8,128)(2,1)}, u32[]{:S(2)}, u32[]{:S(2)}) collective-permute-start(bf16[2048,256]{1,0:T(8,128)(2,1)S(1)} %get-tuple-element.26), channel_id=1, source_target_pairs={{0,0},{1,8},{2,16},{3,24},{4,1},{5,9},{6,17},{7,25},{8,2},{9,10},{... | collective-permute-start | bytes 3145736 | tf_op jit(solution)/shard_map/ppermute | solution.py:181
  6.9 182.6 %collective-permute-start.4 = (bf16[512,2048]{1,0:T(8,128)(2,1)}, bf16[512,2048]{1,0:T(8,128)(2,1)}, u32[]{:S(2)}, u32[]{:S(2)}) collective-permute-start(bf16[512,2048]{1,0:T(8,128)(2,1)} %bitcast.6.refs_2_), channel_id=1, source_target_pairs={{0,1},{1,0},{2,3},{3,2},{4,5},{5,4},{6,7},{7,6},{8,9},{9,8},{10,11... | collective-permute-start | bytes 6291464 | tf_op jit(solution)/shard_map/ppermute | solution.py:193
  7.9 116.1 %collective-permute-start.1 = (bf16[2048,256]{1,0:T(8,128)(2,1)}, bf16[2048,256]{1,0:T(8,128)(2,1)S(1)}, u32[]{:S(2)}, u32[]{:S(2)}) collective-permute-start(bf16[2048,256]{1,0:T(8,128)(2,1)} %get-tuple-element.25), channel_id=1, source_target_pairs={{0,0},{1,8},{2,16},{3,24},{4,1},{5,9},{6,17},{7,25},{8,2},{9,10},{... | collective-permute-start | bytes 3145736 | tf_op jit(solution)/shard_map/ppermute | solution.py:181
  9.7 172.2 %collective-permute-start.10 = (bf16[2048,256]{1,0:T(8,128)(2,1)}, bf16[2048,256]{1,0:T(8,128)(2,1)}, u32[]{:S(2)}, u32[]{:S(2)}) collective-permute-start(bf16[2048,256]{1,0:T(8,128)(2,1)} %collective-permute-done.refs_1_.refs_4_), channel_id=1, source_target_pairs={{0,24},{8,16},{16,8},{24,0},{1,25},{9,17},{17,9},{25,1},{2,26},{10... | collective-permute-start | bytes 3145736 | tf_op jit(solution)/shard_map/ppermute | solution.py:184
  122.1 60.0 %collective-permute-start.8 = (bf16[2048,256]{1,0:T(8,128)(2,1)}, bf16[2048,256]{1,0:T(8,128)(2,1)}, u32[]{:S(2)}, u32[]{:S(2)}) collective-permute-start(bf16[2048,256]{1,0:T(8,128)(2,1)} %collective-permute-done.refs_1_.refs_4_), channel_id=1, source_target_pairs={{0,8},{8,0},{16,24},{24,16},{1,9},{9,1},{17,25},{25,17},{2,10},{10... | collective-permute-start | bytes 3145736 | tf_op jit(solution)/shard_map/ppermute | solution.py:184
  122.1 60.1 %collective-permute-start.9 = (bf16[2048,256]{1,0:T(8,128)(2,1)}, bf16[2048,256]{1,0:T(8,128)(2,1)}, u32[]{:S(2)}, u32[]{:S(2)}) collective-permute-start(bf16[2048,256]{1,0:T(8,128)(2,1)} %collective-permute-done.refs_1_.refs_4_), channel_id=1, source_target_pairs={{0,16},{8,24},{16,0},{24,8},{1,17},{9,25},{17,1},{25,9},{2,18},{10... | collective-permute-start | bytes 3145736 | tf_op jit(solution)/shard_map/ppermute | solution.py:184
  123.9 57.5 %copy-start.12 = (f32[3]{0:T(128)S(1)}, f32[3]{0:T(128)}, u32[]{:S(2)}) copy-start(f32[3]{0:T(128)} %param.6) | copy-start | bytes 40
  123.9 57.9 %copy-start.10 = (f32[2048]{0:T(1024)S(1)}, f32[2048]{0:T(1024)}, u32[]{:S(2)}) copy-start(f32[2048]{0:T(1024)} %param.5) | copy-start | bytes 24580
  123.9 57.9 %copy-start.11 = (f32[3]{0:T(128)S(1)}, f32[3]{0:T(128)}, u32[]{:S(2)}) copy-start(f32[3]{0:T(128)} %param.7) | copy-start | bytes 40
  123.9 192.8 %copy-start = (bf16[2048,256]{1,0:T(8,128)(2,1)}, bf16[2048,256]{1,0:T(8,128)(2,1)S(1)}, u32[]{:S(2)}) copy-start(bf16[2048,256]{1,0:T(8,128)(2,1)S(1)} %collective-permute-done.1.refs_2_.refs_4_.refs_8_) | copy-start | bytes 3145732
  124.0 65.5 %copy-start.1 = (bf16[512,2048]{1,0:T(8,128)(2,1)}, bf16[512,2048]{1,0:T(8,128)(2,1)S(1)}, u32[]{:S(2)}) copy-start(bf16[512,2048]{1,0:T(8,128)(2,1)S(1)} %shard_map.46.refs_8_) | copy-start | bytes 6291460
  124.0 100.7 %collective-permute-start.2 = (bf16[512,2048]{1,0:T(8,128)(2,1)S(1)}, bf16[512,2048]{1,0:T(8,128)(2,1)}, u32[]{:S(2)}, u32[]{:S(2)}) collective-permute-start(bf16[512,2048]{1,0:T(8,128)(2,1)S(1)} %shard_map.46.refs_8_), channel_id=1, source_target_pairs={{2,0},{3,1},{4,2},{5,3},{6,4},{7,5},{0,6},{1,7},{10,8},{11,9},{12,... | collective-permute-start | bytes 6291464 | tf_op jit(solution)/shard_map/ppermute | solution.py:190
  182.0 87.6 %collective-permute-start.3 = (bf16[512,2048]{1,0:T(8,128)(2,1)S(1)}, bf16[512,2048]{1,0:T(8,128)(2,1)S(1)}, u32[]{:S(2)}, u32[]{:S(2)}) collective-permute-start(bf16[512,2048]{1,0:T(8,128)(2,1)S(1)} %shard_map.46.refs_8_), channel_id=1, source_target_pairs={{6,0},{7,1},{0,2},{1,3},{2,4},{3,5},{4,6},{5,7},{14,8},{15,9},{8,1... | collective-permute-start | bytes 6291464 | tf_op jit(solution)/shard_map/ppermute | solution.py:190
  182.1 47.5 %collective-permute-start.5 = (bf16[2048,256]{1,0:T(8,128)(2,1)S(1)}, bf16[2048,256]{1,0:T(8,128)(2,1)S(1)}, u32[]{:S(2)}, u32[]{:S(2)}) collective-permute-start(bf16[2048,256]{1,0:T(8,128)(2,1)S(1)} %collective-permute-done.1.refs_2_.refs_4_.refs_8_), channel_id=1, source_target_pairs={{0,8},{8,0},{16,24},{24,16},{1,9},{9,1},{17,25},{25,17},{2,10},{10... | collective-permute-start | bytes 3145736 | tf_op jit(solution)/shard_map/ppermute | solution.py:184
  182.1 50.2 %collective-permute-start.6 = (bf16[2048,256]{1,0:T(8,128)(2,1)S(1)}, bf16[2048,256]{1,0:T(8,128)(2,1)S(1)}, u32[]{:S(2)}, u32[]{:S(2)}) collective-permute-start(bf16[2048,256]{1,0:T(8,128)(2,1)S(1)} %collective-permute-done.1.refs_2_.refs_4_.refs_8_), channel_id=1, source_target_pairs={{0,16},{8,24},{16,0},{24,8},{1,17},{9,25},{17,1},{25,9},{2,18},{10... | collective-permute-start | bytes 3145736 | tf_op jit(solution)/shard_map/ppermute | solution.py:184
  189.5 42.9 %collective-permute-start.7 = (bf16[2048,256]{1,0:T(8,128)(2,1)S(1)}, bf16[2048,256]{1,0:T(8,128)(2,1)S(1)}, u32[]{:S(2)}, u32[]{:S(2)}) collective-permute-start(bf16[2048,256]{1,0:T(8,128)(2,1)S(1)} %collective-permute-done.1.refs_2_.refs_4_.refs_8_), channel_id=1, source_target_pairs={{0,24},{8,16},{16,8},{24,0},{1,25},{9,17},{17,9},{25,1},{2,26},{10... | collective-permute-start | bytes 3145736 | tf_op jit(solution)/shard_map/ppermute | solution.py:184
  224.7 54.1 %collective-permute-start.13 = (bf16[512,2048]{1,0:T(8,128)(2,1)}, bf16[512,2048]{1,0:T(8,128)(2,1)S(1)}, u32[]{:S(2)}, u32[]{:S(2)}) collective-permute-start(bf16[512,2048]{1,0:T(8,128)(2,1)} %collective-permute-done.2.refs_2_), channel_id=1, source_target_pairs={{0,1},{1,0},{2,3},{3,2},{4,5},{5,4},{6,7},{7,6},{8,9},{9,8},{10,11... | collective-permute-start | bytes 6291464 | tf_op jit(solution)/shard_map/ppermute | solution.py:193
  229.5 25.5 %copy-start.3 = (bf16[2048,256]{1,0:T(8,128)(2,1)}, bf16[2048,256]{1,0:T(8,128)(2,1)S(1)}, u32[]{:S(2)}) copy-start(bf16[2048,256]{1,0:T(8,128)(2,1)S(1)} %collective-permute-done.5.refs_5_.refs_9_) | copy-start | bytes 3145732
  232.3 22.8 %copy-start.4 = (bf16[2048,256]{1,0:T(8,128)(2,1)}, bf16[2048,256]{1,0:T(8,128)(2,1)S(1)}, u32[]{:S(2)}) copy-start(bf16[2048,256]{1,0:T(8,128)(2,1)S(1)} %collective-permute-done.6.refs_6_.refs_10_) | copy-start | bytes 3145732
  232.3 22.8 %copy-start.5 = (bf16[2048,256]{1,0:T(8,128)(2,1)}, bf16[2048,256]{1,0:T(8,128)(2,1)S(1)}, u32[]{:S(2)}) copy-start(bf16[2048,256]{1,0:T(8,128)(2,1)S(1)} %collective-permute-done.7.refs_7_.refs_11_) | copy-start | bytes 3145732
  232.3 37.3 %copy-start.2 = (bf16[512,2048]{1,0:T(8,128)(2,1)S(1)}, bf16[512,2048]{1,0:T(8,128)(2,1)}, u32[]{:S(2)}) copy-start(bf16[512,2048]{1,0:T(8,128)(2,1)} %copy-done.1) | copy-start | bytes 6291460
  269.6 5.1 %copy-start.7 = (bf16[512,2048]{1,0:T(8,128)(2,1)}, bf16[512,2048]{1,0:T(8,128)(2,1)S(1)}, u32[]{:S(2)}) copy-start(bf16[512,2048]{1,0:T(8,128)(2,1)S(1)} %collective-permute-done.3.refs_2_) | copy-start | bytes 6291460
  270.4 46.3 %collective-permute-start.15 = (bf16[256,2048]{1,0:T(8,128)(2,1)S(1)}, bf16[256,2048]{1,0:T(8,128)(2,1)S(1)}, u32[]{:S(2)}, u32[]{:S(2)}) collective-permute-start(bf16[256,2048]{1,0:T(8,128)(2,1)S(1)} %get-tuple-element.23), channel_id=1, source_target_pairs={{2,0},{3,1},{4,6},{5,7},{6,2},{7,3},{0,4},{1,5},{10,8},{11,9},{12,... | collective-permute-start | bytes 3145736 | tf_op jit(solution)/shard_map/ppermute | solution.py:190
  270.5 84.2 %collective-permute-start.11 = (bf16[256,2048]{1,0:T(8,128)(2,1)S(1)}, bf16[256,2048]{1,0:T(8,128)(2,1)S(1)}, u32[]{:S(2)}, u32[]{:S(2)}) collective-permute-start(bf16[256,2048]{1,0:T(8,128)(2,1)S(1)} %get-tuple-element.24), channel_id=1, source_target_pairs={{2,0},{3,1},{4,6},{5,7},{6,2},{7,3},{0,4},{1,5},{10,8},{11,9},{12,... | collective-permute-start | bytes 3145736 | tf_op jit(solution)/shard_map/ppermute | solution.py:190
  274.7 42.0 %collective-permute-start.12 = (bf16[512,2048]{1,0:T(8,128)(2,1)S(1)}, bf16[512,2048]{1,0:T(8,128)(2,1)S(1)}, u32[]{:S(2)}, u32[]{:S(2)}) collective-permute-start(bf16[512,2048]{1,0:T(8,128)(2,1)S(1)} %collective-permute-done.3.refs_2_), channel_id=1, source_target_pairs={{0,1},{1,0},{2,3},{3,2},{4,5},{5,4},{6,7},{7,6},{8,9},{9,8},{10,11... | collective-permute-start | bytes 6291464 | tf_op jit(solution)/shard_map/ppermute | solution.py:193
  278.7 1.3 copy-start.8
  316.7 38.6 %collective-permute-start.16 = (bf16[256,2048]{1,0:T(8,128)(2,1)S(1)}, bf16[256,2048]{1,0:T(8,128)(2,1)S(1)}, u32[]{:S(2)}, u32[]{:S(2)}) collective-permute-start(bf16[256,2048]{1,0:T(8,128)(2,1)S(1)} %shard_map.53.refs_2_), channel_id=1, source_target_pairs={{0,1},{1,0},{2,3},{3,2},{4,5},{5,4},{6,7},{7,6},{8,9},{9,8},{10,11... | collective-permute-start | bytes 3145736 | tf_op jit(solution)/shard_map/ppermute | solution.py:193
  316.8 1.3 copy-start.9
  354.7 21.1 %collective-permute-start.14 = (bf16[256,2048]{1,0:T(8,128)(2,1)S(1)}, bf16[256,2048]{1,0:T(8,128)(2,1)S(1)}, u32[]{:S(2)}, u32[]{:S(2)}) collective-permute-start(bf16[256,2048]{1,0:T(8,128)(2,1)S(1)} %shard_map.52.refs_2_), channel_id=1, source_target_pairs={{0,1},{1,0},{2,3},{3,2},{4,5},{5,4},{6,7},{7,6},{8,9},{9,8},{10,11... | collective-permute-start | bytes 3145736 | tf_op jit(solution)/shard_map/ppermute | solution.py:193

commit v3 on v2

v3 whole, which is shorter than its diff:
```python
import jax
import jax.numpy as jnp
from jax import lax
from jax.experimental import pallas as pl
from jax.experimental.pallas import tpu as pltpu
from jax.sharding import PartitionSpec as P

CHUNK = 512
SUB = 256
STRIP = 16
SLOTS = 3


def gemm_kernel(plan, offs_ref, fac_ref, *refs):
    sizes, first, n_halves, groups, hw, width, n_more, sub = plan
    refs = list(refs)
    row_refs = [refs.pop(0) for _ in sizes]
    col_refs = [refs.pop(0) for _ in range(n_halves)]
    refs = refs[n_more:]
    out_ref, tok_ref = refs.pop(0), refs.pop(0)
    tok_ref[...] = jnp.zeros_like(tok_ref)
    rows_v, cols_v, w_v, o_v, row_sem, col_sem, out_sem = refs
    nt, depth = fac_ref.shape
    starts = [sum(sizes[:p]) for p in range(len(sizes))]
    per = CHUNK // hw
    per_half = groups // per
    chunks = n_halves * per_half
    subs = sum(sizes) // sub
    part = sub // chunks

    def row_copy(p):
        return pltpu.make_async_copy(row_refs[p], rows_v.at[pl.ds(starts[p], sizes[p])], row_sem.at[p])

    def col_copy(h, g, sem_h, sem_g):
        i = offs_ref[subs + g]
        return pltpu.make_async_copy(
            col_refs[h].at[g],
            cols_v.at[h * per_half + i // per, :, pl.ds(pl.multiple_of(lax.rem(i, per) * hw, hw), hw)],
            col_sem.at[sem_h, sem_g],
        )

    row_copy(0).start()
    for h in range(n_halves):
        for g in range(groups):
            col_copy(h, g, h, g).start()
    for p in range(1, len(sizes)):
        row_copy(p).start()

    def weigh(slot, src, dst):
        x = rows_v[pl.ds(src, STRIP), :].astype(jnp.float32)
        for t in range(nt):
            w_v[slot, pl.ds(t * sub + dst, STRIP), :] = (x * fac_ref[pl.ds(t, 1), :]).astype(jnp.bfloat16)

    row_copy(0).wait()

    def weigh_first(k, _):
        at = pl.multiple_of(k * STRIP, STRIP)
        weigh(0, at, at)
        return 0

    lax.fori_loop(0, sub // STRIP, weigh_first, 0)

    def out_copies(slot, s, n):
        h = n // per_half
        i0 = lax.rem(n, per_half) * per
        row0 = pl.multiple_of(offs_ref[s], sub)
        return [
            pltpu.make_async_copy(
                o_v.at[slot, :, :, pl.ds(e * hw, hw)],
                out_ref.at[:, pl.ds(row0, sub), pl.ds(pl.multiple_of((i0 + e) * width + (first + h) * hw, hw), hw)],
                out_sem.at[slot, e],
            )
            for e in range(per)
        ]

    total = subs * chunks

    def step(q, _):
        s, n = q // chunks, lax.rem(q, chunks)
        slot = lax.rem(q, SLOTS)
        cur = lax.rem(s, 2)

        @pl.when(s == 0)
        def _():
            h = n // per_half
            for e in range(per):
                g = offs_ref[subs + lax.rem(n, per_half) * per + e]
                col_copy(0, 0, h, g).wait()

        for p in range(1, len(sizes)):

            @pl.when((n == 0) & (s + 1 == starts[p] // sub))
            def _():
                row_copy(p).wait()

        @pl.when(q >= SLOTS)
        def _():
            for c in out_copies(slot, s, n):
                c.wait()

        src = jnp.minimum(s + 1, subs - 1) * sub + n * part
        for k in range(part // STRIP):
            weigh(1 - cur, pl.multiple_of(src + k * STRIP, STRIP), pl.multiple_of(n * part + k * STRIP, STRIP))
        res = jnp.dot(w_v[cur], cols_v[n], preferred_element_type=jnp.float32)
        o_v[slot] = res.reshape(nt, sub, CHUNK)
        for c in out_copies(slot, s, n):
            c.start()
        return 0

    lax.fori_loop(0, total, step, 0)
    for q in range(max(0, total - SLOTS), total):
        for c in out_copies(q % SLOTS, q // chunks, q % chunks):
            c.wait()


def tie(x, *deps):
    hbm = pl.BlockSpec(memory_space=pl.ANY)
    return pl.pallas_call(
        lambda *refs: None,
        out_shape=jax.ShapeDtypeStruct(x.shape, x.dtype),
        in_specs=[hbm] * (1 + len(deps)),
        out_specs=hbm,
        input_output_aliases={0: 0},
        compiler_params=pltpu.CompilerParams(vmem_limit_bytes=48 * 1024 * 1024),
    )(x, *deps)


def gemm(factors, rows, row_offs, first, halves, shards, out, out_shape, width, deps=()):
    nt, depth = factors.shape
    sizes = [x.shape[0] for x in rows]
    groups, _, hw = halves[0].shape
    sub = min(SUB, *sizes)
    offs = [o + k * sub for o, m in zip(row_offs, sizes) for k in range(m // sub)] + list(shards)
    offs = jnp.stack([jnp.asarray(o, jnp.int32) for o in offs])
    chunks = len(halves) * groups * hw // CHUNK
    plan = (sizes, first, len(halves), groups, hw, width, len(deps) + (out is not None), sub)
    args = [factors, *rows, *halves, *deps]
    hbm = pl.BlockSpec(memory_space=pl.ANY)
    in_specs = [pl.BlockSpec(memory_space=pltpu.VMEM)] + [hbm] * (len(args) - 1)
    aliases = {}
    if out is not None:
        aliases = {len(args) + 1: 0}
        args.append(out)
        in_specs.append(hbm)
    m, n = sum(sizes), len(halves) * groups * hw
    return pl.pallas_call(
        lambda *refs: gemm_kernel(plan, *refs),
        out_shape=(jax.ShapeDtypeStruct(out_shape, jnp.float32), jax.ShapeDtypeStruct((8, 128), jnp.float32)),
        grid_spec=pltpu.PrefetchScalarGridSpec(
            num_scalar_prefetch=1,
            grid=(),
            in_specs=in_specs,
            out_specs=(hbm, pl.BlockSpec(memory_space=pltpu.VMEM)),
            scratch_shapes=[
                pltpu.VMEM((m, depth), jnp.bfloat16),
                pltpu.VMEM((chunks, depth, CHUNK), jnp.bfloat16),
                pltpu.VMEM((2, nt * sub, depth), jnp.bfloat16),
                pltpu.VMEM((SLOTS, nt, sub, CHUNK), jnp.float32),
                pltpu.SemaphoreType.DMA((len(sizes),)),
                pltpu.SemaphoreType.DMA((len(halves), groups)),
                pltpu.SemaphoreType.DMA((SLOTS, CHUNK // hw)),
            ],
        ),
        input_output_aliases=aliases,
        compiler_params=pltpu.CompilerParams(vmem_limit_bytes=48 * 1024 * 1024),
        cost_estimate=pl.CostEstimate(
            flops=2 * nt * m * n * depth,
            bytes_accessed=4 * nt * m * n + 2 * depth * (m + n),
            transcendentals=0,
        ),
    )(offs, *args)


def solution(mesh):
    R, C = mesh.shape["row"], mesh.shape["col"]
    Z = C // 2
    B = C // R

    def on_device(pair_ints, denominators, lap_points, lap_weights):
        depth, width = pair_ints.shape
        u = lax.axis_index("col")
        z, core = u // 2, lax.rem(u, 2)
        factors = lap_weights[:, None] * jnp.exp(-lap_points[:, None] * denominators[None, :])
        nt = factors.shape[0]
        n_halves = 2 if width % 256 == 0 else 1
        hw = width // n_halves
        out_shape = (nt, C * width, R * width)

        def spread(x):
            return lax.ppermute(x, ("row", "col"), [(a * C + b, (a ^ b % R) * C + b) for a in range(R) for b in range(C)])

        def deliver(x):
            return lax.ppermute(
                x, ("row", "col"), [(a * C + b, a * C + (a ^ b % R) * B + b // R) for a in range(R) for b in range(C)]
            )

        def gather(x):
            return lax.all_gather(x, "row", axis=0)

        def col_perm(x, pairs):
            return lax.ppermute(x, "col", [(2 * a + k, 2 * b + k) for a, b in pairs for k in range(2)])

        def swap(x):
            return lax.ppermute(x, "col", [(a, a ^ 1) for a in range(C)])

        shards = [g ^ (u // B) for g in range(R)]

        def block(pieces, first, hs, out, deps=()):
            rows, offs = [], []
            for x, swapped, where, extra in pieces:
                rows += [x, swapped]
                offs += [(2 * where + core) * width + extra, (2 * where + 1 - core) * width + extra]
            return gemm(factors, rows, offs, first, hs, shards, out, out_shape, width, deps)

        mine = pair_ints.T
        own = (mine, swap(mine), z, 0)
        if Z != 4 or n_halves != 2:
            halves = [gather(deliver(spread(pair_ints[:, h * hw : (h + 1) * hw]))) for h in range(n_halves)]
            out, _ = block([own], 0, halves, None)
            for d in range(1, Z):
                x = col_perm(mine, [((a + d) % Z, a) for a in range(Z)])
                out, _ = block([(x, swap(x), lax.rem(z + d, Z), 0)], 0, halves, out)
            return out

        m2 = width // 2
        nxt = [((a + 1) % Z, a) for a in range(Z)]
        prv = [((a - 1) % Z, a) for a in range(Z)]
        up_a = col_perm(mine[:m2], nxt)
        sent_a = spread(pair_ints[:, :hw])
        sent_b = spread(tie(pair_ints[:, hw:], sent_a))
        got_a = deliver(tie(sent_a, up_a))
        got_b = deliver(sent_b)
        cols_a, cols_b = gather(got_a), gather(got_b)
        late = tie(mine, got_a)
        up_b = col_perm(late[m2:], nxt)
        late = tie(late, got_b)
        down = col_perm(late, prv)

        one = lax.rem(z + 1, Z)
        ups = [(up_a, swap(up_a), one, 0), (up_b, swap(up_b), one, m2)]
        out, token = block([own], 0, [cols_a], None, (late,))
        out, token = block(ups, 0, [cols_a], out)
        up = jnp.concatenate([up_a, up_b])
        down = tie(down, token)
        fwd = jnp.where(z == 1, up, jnp.where(z == 2, down, late))
        pairs = [(1, 0), (2, 3), (3, 1), (0, 2)]
        last = [col_perm(fwd[:m2], pairs), col_perm(fwd[m2:], pairs)]
        out, token_b = block([own] + ups, 1, [cols_b], out, (fwd,))
        halves = [cols_a, cols_b]
        out, token_d = block([(down, swap(down), lax.rem(z + 3, Z), 0)], 0, halves, out)
        for k, token in enumerate((token_b, token_d)):
            x = tie(last[k], token)
            out, _ = block([(x, swap(x), lax.rem(z + 2, Z), k * m2)], 0, halves, out)
        return out

    in_specs = (P(None, ("row", "col")), P(), P(), P())
    out_specs = P(None, "row", "col")
    return jax.shard_map(on_device, mesh=mesh, in_specs=in_specs, out_specs=out_specs, check_vma=False)
```

time: 397 us -> 379 us (0.955)
  the two profiles are of different devices: /device:TPU:31 before, /device:TPU:29 now
where the time goes in v3:
time: 379 us
  Pallas kernels  157 us (41%)
  waiting for transfers between devices  105 us (28%)
  starting transfers between devices  82.1 us (22%)
  local copies, waits for them, and re-layouts  18.4 us (5%)
  between operations  13.7 us (4%)
    pallas_call x6, Pallas kernels, gemm(): pl.pallas_call(lambda *refs: gemm_kernel(plan, *refs), out_shape=(jax.Sha...  157 us
    ppermute x5, starting transfers between devices, col_perm(): lax.ppermute(x, 'col', [(2 * a + k, 2 * b + k) for a, b in pairs for k in...  51.5 us
    ppermute x5, waiting for transfers between devices, col_perm(): lax.ppermute(x, 'col', [(2 * a + k, 2 * b + k) for a, b in pairs for k in...  39.2 us
    ppermute x2, waiting for transfers between devices, deliver(): lax.ppermute(x, ('row', 'col'), [(a * C + b, a * C + (a ^ b % R) * B + b...  35.3 us
    ppermute x2, waiting for transfers between devices, spread(): lax.ppermute(x, ('row', 'col'), [(a * C + b, (a ^ b % R) * C + b) for a i...  30.1 us
    ppermute x6, starting transfers between devices, swap(): return lax.ppermute(x, 'col', [(a, a ^ 1) for a in range(C)])  15.6 us
    unnamed x24, local copies, waits for them, and re-layouts  11.1 us
    ppermute x2, starting transfers between devices, deliver(): lax.ppermute(x, ('row', 'col'), [(a * C + b, a * C + (a ^ b % R) * B + b...  9.92 us
  transfers between devices with their start and end apart: 17, of which 7 were waited for; matrix products, arithmetic and copies ran while one was open for 3% of the time, Pallas kernels for 36%

profile of v3, /device:TPU:29, one launch (start us, length us, event | category | flops | bytes accessed | tf_op | source)
XLA Modules:
  0.0 378.7 jit_solution(7543456020772987812)
XLA Ops:
  6.5 2.6 fusion.1
  9.2 3.0 collective-permute-start.1
  12.2 4.0 %copy.17 = bf16[2048,512]{0,1:T(8,128)(2,1)} copy(bf16[2048,512]{1,0:T(8,128)(2,1)} %param.4) | data formatting | bytes 4194304 | tf_op args[0]
  16.2 1.3 slice.24
  17.8 8.3 %collective-permute-done.1.refs_0_.refs_1_ = bf16[2048,256]{1,0:T(8,128)(2,1)S(1)} collective-permute-done((bf16[2048,256]{1,0:T(8,128)(2,1)}, bf16[2048,256]{1,0:T(8,128)(2,1)S(1)}, u32[]{:S(2)}, u32[]{:S(2)}) %collective-permute-start.1) | collective-permute-done | bytes 1048608 | tf_op jit(solution)/shard_map/ppermute | solution.py:190
  26.2 1.0 copy-done.6
  27.2 17.0 %collective-permute-done.refs_1_.refs_2_.refs_4_ = bf16[256,2048]{1,0:T(8,128)(2,1)S(1)} collective-permute-done((bf16[256,2048]{1,0:T(8,128)(2,1)S(1)}, bf16[256,2048]{1,0:T(8,128)(2,1)S(1)}, u32[]{:S(2)}, u32[]{:S(2)}) %collective-permute-start) | collective-permute-done | bytes 1048608 | tf_op jit(solution)/shard_map/ppermute | solution.py:201
  44.2 1.9 collective-permute-start.2
  46.1 22.6 %collective-permute-done.2.refs_1_ = bf16[2048,256]{1,0:T(8,128)(2,1)S(1)} collective-permute-done((bf16[2048,256]{1,0:T(8,128)(2,1)S(1)}, bf16[2048,256]{1,0:T(8,128)(2,1)S(1)}, u32[]{:S(2)}, u32[]{:S(2)}) %collective-permute-start.2) | collective-permute-done | bytes 1048608 | tf_op jit(solution)/shard_map/ppermute | solution.py:193
  68.7 1.0 copy-done.4
  69.7 1.9 collective-permute-start.4
  71.6 21.8 %collective-permute-done.4 = bf16[2048,256]{1,0:T(8,128)(2,1)S(1)} collective-permute-done((bf16[2048,256]{1,0:T(8,128)(2,1)}, bf16[2048,256]{1,0:T(8,128)(2,1)S(1)}, u32[]{:S(2)}, u32[]{:S(2)}) %collective-permute-start.4) | collective-permute-done | bytes 1048608 | tf_op jit(solution)/shard_map/ppermute | solution.py:190
  93.4 8.0 %collective-permute-start.5 = (bf16[2048,256]{1,0:T(8,128)(2,1)S(1)}, bf16[2048,256]{1,0:T(8,128)(2,1)S(1)}, u32[]{:S(2)}, u32[]{:S(2)}) collective-permute-start(bf16[2048,256]{1,0:T(8,128)(2,1)S(1)} %collective-permute-done.4), channel_id=1, source_target_pairs={{0,0},{1,2},{2,4},{3,6},{4,1},{5,3},{6,5},{7,7},{8,10},{9,8},{10,1... | collective-permute-start | bytes 3145736 | tf_op jit(solution)/shard_map/ppermute | solution.py:193
  101.5 12.7 %collective-permute-done.5.refs_1_ = bf16[2048,256]{1,0:T(8,128)(2,1)S(1)} collective-permute-done((bf16[2048,256]{1,0:T(8,128)(2,1)S(1)}, bf16[2048,256]{1,0:T(8,128)(2,1)S(1)}, u32[]{:S(2)}, u32[]{:S(2)}) %collective-permute-start.5) | collective-permute-done | bytes 1048608 | tf_op jit(solution)/shard_map/ppermute | solution.py:193
  114.2 1.0 copy-done.2
  115.2 13.3 %collective-permute-start.9 = (bf16[512,2048]{1,0:T(8,128)(2,1)}, bf16[512,2048]{1,0:T(8,128)(2,1)}, u32[]{:S(2)}, u32[]{:S(2)}) collective-permute-start(bf16[512,2048]{1,0:T(8,128)(2,1)} %bitcast.6.refs_2_), channel_id=1, source_target_pairs={{0,1},{1,0},{2,3},{3,2},{4,5},{5,4},{6,7},{7,6},{8,9},{9,8},{10,11... | collective-permute-start | bytes 6291464 | tf_op jit(solution)/shard_map/ppermute | solution.py:204
  128.5 1.6 copy.19.refs_0_
  130.1 1.0 slice.25
  132.1 1.2 copy-done.3
  133.3 8.2 %collective-permute-start.6 = (bf16[512,2048]{1,0:T(8,128)(2,1)S(1)}, bf16[512,2048]{1,0:T(8,128)(2,1)}, u32[]{:S(2)}, u32[]{:S(2)}) collective-permute-start(bf16[512,2048]{1,0:T(8,128)(2,1)S(1)} %shard_map.49.refs_5_), channel_id=1, source_target_pairs={{6,0},{7,1},{0,2},{1,3},{2,4},{3,5},{4,6},{5,7},{14,8},{15,9},{8,1... | collective-permute-start | bytes 6291464 | tf_op jit(solution)/shard_map/ppermute | solution.py:201
  141.5 21.7 %collective-permute-done.3.refs_4_.refs_6_ = bf16[256,2048]{1,0:T(8,128)(2,1)} collective-permute-done((bf16[256,2048]{1,0:T(8,128)(2,1)}, bf16[256,2048]{1,0:T(8,128)(2,1)}, u32[]{:S(2)}, u32[]{:S(2)}) %collective-permute-start.3) | collective-permute-done | bytes 1048608 | tf_op jit(solution)/shard_map/ppermute | solution.py:201
  164.1 22.3 %shard_map.50 = (f32[3,4096,2048]{2,1,0:T(8,128)}, f32[8,128]{1,0:T(8,128)}) custom-call(s32[8]{0:T(128)S(1)} %stack.122.refs_0_, f32[3,2048]{1,0:T(4,128)S(1)} %exponential_multiply_fusion.refs_1_, bf16[512,2048]{1,0:T(8,128)(2,1)} %bitcast.6.refs_2_, bf16[512,2048]{1,0:T(8,128)(2,1)} %collective-permute-done.9.refs_3_, bf16[4,2048,256]{2,1,0:T(8,128)(2,1)} %bitcast.23, ...), custom_call_target="tpu_custom_call" | custom-call | flops 12884901888 | bytes 20971520 | tf_op jit(solution)/shard_map/pallas_call | solution.py:146
  186.4 21.3 %shard_map.51 = (f32[3,4096,2048]{2,1,0:T(8,128)}, f32[8,128]{1,0:T(8,128)S(1)}) custom-call(s32[8]{0:T(128)S(1)} %stack.117.refs_0_, f32[3,2048]{1,0:T(4,128)S(1)} %exponential_multiply_fusion.refs_1_, bf16[256,2048]{1,0:T(8,128)(2,1)S(1)} %collective-permute-done.refs_1_.refs_2_.refs_4_, ...), custom_call_target="tpu_custom_call", output_to_operand_aliasing={{0}: (7, {})} | custom-call | flops 12884901888 | bytes 20971520 | tf_op jit(solution)/shard_map/pallas_call | solution.py:146
  208.7 1.2 copy-done.1
  209.9 2.7 maximum_select_fusion.refs_9_
  212.6 1.8 fusion
  214.5 40.8 %collective-permute-start.13 = (bf16[256,2048]{1,0:T(8,128)(2,1)}, bf16[256,2048]{1,0:T(8,128)(2,1)S(1)}, u32[]{:S(2)}, u32[]{:S(2)}) collective-permute-start(bf16[256,2048]{1,0:T(8,128)(2,1)} %get-tuple-element.23), channel_id=1, source_target_pairs={{2,0},{3,1},{4,6},{5,7},{6,2},{7,3},{0,4},{1,5},{10,8},{11,9},{12,... | collective-permute-start | bytes 3145736 | tf_op jit(solution)/shard_map/ppermute | solution.py:201
  255.4 2.2 collective-permute-start.10
  257.6 37.8 %shard_map.53 = (f32[3,4096,2048]{2,1,0:T(8,128)}, f32[8,128]{1,0:T(8,128)S(1)}) custom-call(s32[12]{0:T(128)S(1)} %stack.128.refs_0_, f32[3,2048]{1,0:T(4,128)S(1)} %exponential_multiply_fusion.refs_1_, bf16[512,2048]{1,0:T(8,128)(2,1)} %bitcast.6.refs_2_, bf16[512,2048]{1,0:T(8,128)(2,1)} %collective-permute-done.9.refs_3_, ...), custom_call_target="tpu_custom_call", output_to_operand_aliasing={{0}: (10, {})} | custom-call | flops 25769803776 | bytes 37748736 | tf_op jit(solution)/shard_map/pallas_call | solution.py:146
  296.1 35.7 %shard_map.54 = (f32[3,4096,2048]{2,1,0:T(8,128)}, f32[8,128]{1,0:T(8,128)S(1)}) custom-call(s32[8]{0:T(128)S(1)} %stack.127.refs_0_, f32[3,2048]{1,0:T(4,128)S(1)} %exponential_multiply_fusion.refs_1_, bf16[512,2048]{1,0:T(8,128)(2,1)} %shard_map.52.refs_2_, bf16[512,2048]{1,0:T(8,128)(2,1)} %collective-permute-done.11.refs_3_, ...), custom_call_target="tpu_custom_call", output_to_operand_aliasing={{0}: (6, {})} | custom-call | flops 25769803776 | bytes 37748736 | tf_op jit(solution)/shard_map/pallas_call | solution.py:146
  331.9 20.0 %shard_map.57 = (f32[3,4096,2048]{2,1,0:T(8,128)}, f32[8,128]{1,0:T(8,128)}) custom-call(s32[6]{0:T(128)S(1)} %stack.131.refs_0_, f32[3,2048]{1,0:T(4,128)S(1)} %exponential_multiply_fusion.refs_1_, bf16[256,2048]{1,0:T(8,128)(2,1)S(1)} %shard_map.56.refs_2_, bf16[256,2048]{1,0:T(8,128)(2,1)S(1)} %collective-permute-done.14.refs_3_, ...), custom_call_target="tpu_custom_call", output_to_operand_aliasing={{0}: (6, {})} | custom-call | flops 12884901888 | bytes 23068672 | tf_op jit(solution)/shard_map/pallas_call | solution.py:146
  351.9 20.0 %shard_map.58 = (f32[3,4096,2048]{2,1,0:T(8,128)}, f32[8,128]{1,0:T(8,128)}) custom-call(s32[6]{0:T(128)S(1)} %stack.112.refs_0_, f32[3,2048]{1,0:T(4,128)S(1)} %exponential_multiply_fusion.refs_1_, bf16[256,2048]{1,0:T(8,128)(2,1)S(1)} %shard_map.55.refs_2_, bf16[256,2048]{1,0:T(8,128)(2,1)S(1)} %collective-permute-done.12.refs_3_, ...), custom_call_target="tpu_custom_call", output_to_operand_aliasing={{0}: (6, {})} | custom-call | flops 12884901888 | bytes 23068672 | tf_op jit(solution)/shard_map/pallas_call | solution.py:146
  (54 shorter events, 4.1 us)
Async XLA Ops:
  6.5 157.6 %all-gather.5.cloned.1.call-start = ((), (), s32[]{:S(2)}) async-start(), calls=%async_computation | async-start | bytes 5242880 | tf_op jit(solution)/shard_map/all_gather | solution.py:198
  9.2 17.0 %collective-permute-start.1 = (bf16[2048,256]{1,0:T(8,128)(2,1)}, bf16[2048,256]{1,0:T(8,128)(2,1)S(1)}, u32[]{:S(2)}, u32[]{:S(2)}) collective-permute-start(bf16[2048,256]{1,0:T(8,128)(2,1)} %get-tuple-element.26), channel_id=1, source_target_pairs={{0,0},{1,9},{2,18},{3,27},{4,4},{5,13},{6,22},{7,31},{8,8},{9,1},{... | collective-permute-start | bytes 3145736 | tf_op jit(solution)/shard_map/ppermute | solution.py:190
  17.5 26.6 %collective-permute-start = (bf16[256,2048]{1,0:T(8,128)(2,1)S(1)}, bf16[256,2048]{1,0:T(8,128)(2,1)S(1)}, u32[]{:S(2)}, u32[]{:S(2)}) collective-permute-start(bf16[256,2048]{1,0:T(8,128)(2,1)S(1)} %slice.24), channel_id=1, source_target_pairs={{2,0},{3,1},{4,2},{5,3},{6,4},{7,5},{0,6},{1,7},{10,8},{11,9},{12,... | collective-permute-start | bytes 3145736 | tf_op jit(solution)/shard_map/ppermute | solution.py:201
  26.2 1.0 copy-start.6
  44.2 24.5 %collective-permute-start.2 = (bf16[2048,256]{1,0:T(8,128)(2,1)S(1)}, bf16[2048,256]{1,0:T(8,128)(2,1)S(1)}, u32[]{:S(2)}, u32[]{:S(2)}) collective-permute-start(bf16[2048,256]{1,0:T(8,128)(2,1)S(1)} %shard_map.46), channel_id=1, source_target_pairs={{0,0},{1,2},{2,4},{3,6},{4,1},{5,3},{6,5},{7,7},{8,10},{9,8},{10,1... | collective-permute-start | bytes 3145736 | tf_op jit(solution)/shard_map/ppermute | solution.py:193
  68.7 1.0 copy-start.4
  69.7 187.9 %all-gather.7.cloned.1.call-start = ((), (), s32[]{:S(2)}) async-start(), calls=%async_computation.1 | async-start | bytes 5242880 | tf_op jit(solution)/shard_map/all_gather | solution.py:198
  69.7 23.7 %collective-permute-start.4 = (bf16[2048,256]{1,0:T(8,128)(2,1)}, bf16[2048,256]{1,0:T(8,128)(2,1)S(1)}, u32[]{:S(2)}, u32[]{:S(2)}) collective-permute-start(bf16[2048,256]{1,0:T(8,128)(2,1)} %copy-done.6), channel_id=1, source_target_pairs={{0,0},{1,9},{2,18},{3,27},{4,4},{5,13},{6,22},{7,31},{8,8},{9,1},{... | collective-permute-start | bytes 3145736 | tf_op jit(solution)/shard_map/ppermute | solution.py:190
  93.4 20.8 %collective-permute-start.5 = (bf16[2048,256]{1,0:T(8,128)(2,1)S(1)}, bf16[2048,256]{1,0:T(8,128)(2,1)S(1)}, u32[]{:S(2)}, u32[]{:S(2)}) collective-permute-start(bf16[2048,256]{1,0:T(8,128)(2,1)S(1)} %collective-permute-done.4), channel_id=1, source_target_pairs={{0,0},{1,2},{2,4},{3,6},{4,1},{5,3},{6,5},{7,7},{8,10},{9,8},{10,1... | collective-permute-start | bytes 3145736 | tf_op jit(solution)/shard_map/ppermute | solution.py:193
  114.2 1.0 copy-start.2
  115.2 14.9 %copy-start.5 = (bf16[2048,256]{1,0:T(8,128)(2,1)S(1)}, bf16[2048,256]{1,0:T(8,128)(2,1)}, u32[]{:S(2)}) copy-start(bf16[2048,256]{1,0:T(8,128)(2,1)} %copy-done.4) | copy-start | bytes 3145732
  115.2 48.9 %collective-permute-start.9 = (bf16[512,2048]{1,0:T(8,128)(2,1)}, bf16[512,2048]{1,0:T(8,128)(2,1)}, u32[]{:S(2)}, u32[]{:S(2)}) collective-permute-start(bf16[512,2048]{1,0:T(8,128)(2,1)} %bitcast.6.refs_2_), channel_id=1, source_target_pairs={{0,1},{1,0},{2,3},{3,2},{4,5},{5,4},{6,7},{7,6},{8,9},{9,8},{10,11... | collective-permute-start | bytes 6291464 | tf_op jit(solution)/shard_map/ppermute | solution.py:204
  130.1 1.3 copy-start.10
  130.1 1.6 copy-start.8
  130.1 1.6 copy-start.9
  131.1 32.0 %collective-permute-start.3 = (bf16[256,2048]{1,0:T(8,128)(2,1)}, bf16[256,2048]{1,0:T(8,128)(2,1)}, u32[]{:S(2)}, u32[]{:S(2)}) collective-permute-start(bf16[256,2048]{1,0:T(8,128)(2,1)} %slice.25), channel_id=1, source_target_pairs={{2,0},{3,1},{4,2},{5,3},{6,4},{7,5},{0,6},{1,7},{10,8},{11,9},{12,... | collective-permute-start | bytes 3145736 | tf_op jit(solution)/shard_map/ppermute | solution.py:201
  131.8 54.6 %collective-permute-start.7 = (bf16[256,2048]{1,0:T(8,128)(2,1)S(1)}, bf16[256,2048]{1,0:T(8,128)(2,1)}, u32[]{:S(2)}, u32[]{:S(2)}) collective-permute-start(bf16[256,2048]{1,0:T(8,128)(2,1)S(1)} %collective-permute-done.refs_1_.refs_2_.refs_4_), channel_id=1, source_target_pairs={{0,1},{1,0},{2,3},{3,2},{4,5},{5,4},{6,7},{7,6},{8,9},{9,8},{10,11... | collective-permute-start | bytes 3145736 | tf_op jit(solution)/shard_map/ppermute | solution.py:204
  132.1 1.2 copy-start.3
  133.3 30.8 %copy-start = (bf16[512,2048]{1,0:T(8,128)(2,1)}, bf16[512,2048]{1,0:T(8,128)(2,1)S(1)}, u32[]{:S(2)}) copy-start(bf16[512,2048]{1,0:T(8,128)(2,1)S(1)} %shard_map.49.refs_5_) | copy-start | bytes 6291460
  133.3 75.0 %collective-permute-start.6 = (bf16[512,2048]{1,0:T(8,128)(2,1)S(1)}, bf16[512,2048]{1,0:T(8,128)(2,1)}, u32[]{:S(2)}, u32[]{:S(2)}) collective-permute-start(bf16[512,2048]{1,0:T(8,128)(2,1)S(1)} %shard_map.49.refs_5_), channel_id=1, source_target_pairs={{6,0},{7,1},{0,2},{1,3},{2,4},{3,5},{4,6},{5,7},{14,8},{15,9},{8,1... | collective-permute-start | bytes 6291464 | tf_op jit(solution)/shard_map/ppermute | solution.py:201
  163.2 23.2 %collective-permute-start.8 = (bf16[256,2048]{1,0:T(8,128)(2,1)}, bf16[256,2048]{1,0:T(8,128)(2,1)}, u32[]{:S(2)}, u32[]{:S(2)}) collective-permute-start(bf16[256,2048]{1,0:T(8,128)(2,1)} %collective-permute-done.3.refs_4_.refs_6_), channel_id=1, source_target_pairs={{0,1},{1,0},{2,3},{3,2},{4,5},{5,4},{6,7},{7,6},{8,9},{9,8},{10,11... | collective-permute-start | bytes 3145736 | tf_op jit(solution)/shard_map/ppermute | solution.py:204
  208.3 1.6 copy-start.1
  208.3 87.8 %collective-permute-start.11 = (bf16[512,2048]{1,0:T(8,128)(2,1)}, bf16[512,2048]{1,0:T(8,128)(2,1)}, u32[]{:S(2)}, u32[]{:S(2)}) collective-permute-start(bf16[512,2048]{1,0:T(8,128)(2,1)} %shard_map.52.refs_2_), channel_id=1, source_target_pairs={{0,1},{1,0},{2,3},{3,2},{4,5},{5,4},{6,7},{7,6},{8,9},{9,8},{10,11... | collective-permute-start | bytes 6291464 | tf_op jit(solution)/shard_map/ppermute | solution.py:204
  212.6 2.0 copy-start.7
  214.5 80.8 %collective-permute-start.13 = (bf16[256,2048]{1,0:T(8,128)(2,1)}, bf16[256,2048]{1,0:T(8,128)(2,1)S(1)}, u32[]{:S(2)}, u32[]{:S(2)}) collective-permute-start(bf16[256,2048]{1,0:T(8,128)(2,1)} %get-tuple-element.23), channel_id=1, source_target_pairs={{2,0},{3,1},{4,6},{5,7},{6,2},{7,3},{0,4},{1,5},{10,8},{11,9},{12,... | collective-permute-start | bytes 3145736 | tf_op jit(solution)/shard_map/ppermute | solution.py:201
  255.4 76.4 %collective-permute-start.10 = (bf16[256,2048]{1,0:T(8,128)(2,1)}, bf16[256,2048]{1,0:T(8,128)(2,1)S(1)}, u32[]{:S(2)}, u32[]{:S(2)}) collective-permute-start(bf16[256,2048]{1,0:T(8,128)(2,1)} %get-tuple-element.24), channel_id=1, source_target_pairs={{2,0},{3,1},{4,6},{5,7},{6,2},{7,3},{0,4},{1,5},{10,8},{11,9},{12,... | collective-permute-start | bytes 3145736 | tf_op jit(solution)/shard_map/ppermute | solution.py:201
  295.4 36.5 %collective-permute-start.14 = (bf16[256,2048]{1,0:T(8,128)(2,1)S(1)}, bf16[256,2048]{1,0:T(8,128)(2,1)S(1)}, u32[]{:S(2)}, u32[]{:S(2)}) collective-permute-start(bf16[256,2048]{1,0:T(8,128)(2,1)S(1)} %shard_map.56.refs_2_), channel_id=1, source_target_pairs={{0,1},{1,0},{2,3},{3,2},{4,5},{5,4},{6,7},{7,6},{8,9},{9,8},{10,11... | collective-permute-start | bytes 3145736 | tf_op jit(solution)/shard_map/ppermute | solution.py:204
  331.8 20.1 %collective-permute-start.12 = (bf16[256,2048]{1,0:T(8,128)(2,1)S(1)}, bf16[256,2048]{1,0:T(8,128)(2,1)S(1)}, u32[]{:S(2)}, u32[]{:S(2)}) collective-permute-start(bf16[256,2048]{1,0:T(8,128)(2,1)S(1)} %shard_map.55.refs_2_), channel_id=1, source_target_pairs={{0,1},{1,0},{2,3},{3,2},{4,5},{5,4},{6,7},{7,6},{8,9},{9,8},{10,11... | collective-permute-start | bytes 3145736 | tf_op jit(solution)/shard_map/ppermute | solution.py:204
Sparse Core Ops, SparseCore 0:
  69.8 64.2 all-gather.4
  135.9 52.6 all-gather.6
